TPU v7x, 256 devices: a whole 4x4x8 slice. The times are simulated.
256 devices in a mesh: slab: 8 (over y, core), head: 32 (over z, x).
Axes of the slice: x: 4, y: 4, z: 8, core: 2. Of those that a mesh axis runs over, the one named last changes fastest.
Arguments:
- queries: bfloat16 [32768, 4096], P(('slab', 'head')), may hold values from -500 to 500
- keys: bfloat16 [32768, 4096], P(('slab', 'head')), may hold values from -500 to 500
- values: bfloat16 [32768, 4096], P(('slab', 'head')), may hold values from -6 to 6
- q_gain: float32 [128], replicated, may hold values from 0.25 to 1.75
- k_gain: float32 [128], replicated, may hold values from 0.25 to 1.75
- windows: int32 [32, 3], P('head'), may hold values from 0 to 1, as said below
Outputs:
- attended: bfloat16 [32768, 4096], P(('slab', 'head'))
Inputs may be any that keep to these rules, and one draw needn't show every extreme that they name: `windows`: some head has all three extents 1 and some head all three 0.
All inputs are finite; a program needn't handle non-finite values.
Results may differ from a plain program's by a relative error of at most 0.0067.
Values may be sent and summed in bfloat16 or wider, within the bound.
No kernel may reach another device: no remote copies, remote signals or barrier semaphores. Data moves between devices by JAX's collectives and lax.ppermute only.
A program may use at most 192 MiB of HBM per device.

v0:
```python
import functools
import math

import jax
import jax.numpy as jnp
from jax import lax
from jax.experimental import pallas as pl
from jax.experimental.pallas import tpu as pltpu
from jax.sharding import PartitionSpec as P

TILE = 128
HEADS_PER_STEP = 4
VMEM_LIMIT = 48 * 2**20
F32 = jnp.float32
BF16 = jnp.bfloat16


def normed(block, gain):
    widened = block.astype(F32)
    mean_sq = jnp.mean(widened * widened, axis=-1, keepdims=True)
    return (widened * lax.rsqrt(mean_sq + 1e-06) * gain).astype(BF16)


def prep_kv_kernel(keys_ref, values_ref, gain_ref, out_ref):
    gain = gain_ref[...]
    for index in range(HEADS_PER_STEP):
        columns = slice(index * TILE, (index + 1) * TILE)
        out_ref[index, 0] = normed(keys_ref[:, columns], gain)
        out_ref[index, 1] = values_ref[:, columns]


def prep_q_kernel(queries_ref, gain_ref, out_ref):
    gain = gain_ref[...] * (math.log2(math.e) / math.sqrt(TILE))
    for index in range(HEADS_PER_STEP):
        columns = slice(index * TILE, (index + 1) * TILE)
        out_ref[index] = normed(queries_ref[:, columns], gain)


def merge_kernel(heads_ref, out_ref):
    for index in range(HEADS_PER_STEP):
        out_ref[:, index * TILE : (index + 1) * TILE] = heads_ref[index]


def prep_kv(keys, values, gain):
    steps = keys.shape[1] // (TILE * HEADS_PER_STEP)
    wide = pl.BlockSpec((TILE, TILE * HEADS_PER_STEP), lambda i: (0, i))
    return pl.pallas_call(
        prep_kv_kernel,
        grid=(steps,),
        in_specs=[wide, wide, pl.BlockSpec((1, TILE), lambda i: (0, 0))],
        out_specs=pl.BlockSpec((HEADS_PER_STEP, 2, TILE, TILE), lambda i: (i, 0, 0, 0)),
        out_shape=jax.ShapeDtypeStruct((steps * HEADS_PER_STEP, 2, TILE, TILE), BF16),
    )(keys, values, gain.reshape(1, TILE))


def prep_q(queries, gain):
    steps = queries.shape[1] // (TILE * HEADS_PER_STEP)
    return pl.pallas_call(
        prep_q_kernel,
        grid=(steps,),
        in_specs=[
            pl.BlockSpec((TILE, TILE * HEADS_PER_STEP), lambda i: (0, i)),
            pl.BlockSpec((1, TILE), lambda i: (0, 0)),
        ],
        out_specs=pl.BlockSpec((HEADS_PER_STEP, TILE, TILE), lambda i: (i, 0, 0)),
        out_shape=jax.ShapeDtypeStruct((steps * HEADS_PER_STEP, TILE, TILE), BF16),
    )(queries, gain.reshape(1, TILE))


def merge_heads(heads):
    steps = heads.shape[0] // HEADS_PER_STEP
    return pl.pallas_call(
        merge_kernel,
        grid=(steps,),
        in_specs=[pl.BlockSpec((HEADS_PER_STEP, TILE, TILE), lambda i: (i, 0, 0))],
        out_specs=pl.BlockSpec((TILE, TILE * HEADS_PER_STEP), lambda i: (0, i)),
        out_shape=jax.ShapeDtypeStruct((TILE, heads.shape[0] * TILE), BF16),
    )(heads)


def attend_kernel(
    slab_ref, windows_ref, q_ref, kv_ref, low_ref, high_ref, out_ref, sums, *, last_slab
):
    half_r, half_c = pl.program_id(0), pl.program_id(1)
    outer_r, inner_r, extra_r, first_r = 3 * half_r, 1 + half_r, 2 - half_r, 2 * half_r
    outer_c, inner_c, extra_c, first_c = 3 * half_c, 1 + half_c, 2 - half_c, 2 * half_c
    places = [(outer_r, outer_c), (outer_r, inner_c), (inner_r, outer_c), (inner_r, inner_c)]
    shared_r, shared_c = (first_r, first_r + 1), (first_c, first_c + 1)
    wide_t, wide_r, wide_c = (windows_ref[0, axis] >= 1 for axis in range(3))
    everything = wide_t & wide_r & wide_c
    has_low = slab_ref[0] > 0
    has_high = slab_ref[0] < last_slab
    groups = [
        ([0, 1, 2, 3], [(r, c) for r in shared_r for c in shared_c], None),
        ([1, 3], [(r, extra_c) for r in shared_r], wide_c),
        ([2, 3], [(extra_r, c) for c in shared_c], wide_r),
        ([3], [(extra_r, extra_c)], wide_r & wide_c),
    ]
    parts = [((1, 2), (0, 1), None), ((0,), (0,), has_low), ((3,), (1,), has_high)]

    def frame(index):
        if index == 0:
            return low_ref, 0
        if index == 3:
            return high_ref, 0
        return kv_ref, (index - 1) * 16

    def stack(blocks):
        return blocks[0] if len(blocks) == 1 else jnp.concatenate(blocks, axis=0)

    def bias(query, key):
        (place, t), (f, r, c) = query, key
        query_r, query_c = places[place]
        inside = wide_t if f - 1 != t else None
        for wide, a, b in ((wide_r, query_r, r), (wide_c, query_c, c)):
            near = wide | (a == b)
            inside = near if inside is None else inside & near
        return jnp.where(inside, 0.0, -1e30).astype(F32)

    def add(query_list, key_list, masked, first):
        q = stack([q_ref[(t * 4 + places[i][0]) * 4 + places[i][1]] for i, t in query_list])
        total = None
        for start in range(0, len(key_list), 2):
            chunk = key_list[start : start + 2]
            found = [(frame(f), r * 4 + c) for f, r, c in chunk]
            k = stack([ref[base + at, 0] for (ref, base), at in found])
            v = stack([ref[base + at, 1] for (ref, base), at in found])
            scores = lax.dot_general(q, k, (((1,), (1,)), ((), ())), preferred_element_type=F32)
            if masked:
                scores = scores + stack(
                    [
                        jnp.concatenate(
                            [jnp.full((TILE, TILE), bias(query, key)) for key in chunk], axis=1
                        )
                        for query in query_list
                    ]
                )
            weights = jnp.exp2(scores).astype(BF16)
            widened = jnp.concatenate([v, jnp.ones(v.shape, BF16)], axis=1)
            part = jnp.dot(weights, widened, preferred_element_type=F32)
            total = part if total is None else total + part
        for n, (i, t) in enumerate(query_list):
            rows = total[n * TILE : (n + 1) * TILE]
            if first:
                sums[i * 2 + t] = rows
            else:
                sums[i * 2 + t] += rows

    def run(masked):
        for frames, times, present in parts:
            for query_places, key_places, needed in groups:
                conditions = [] if present is None else [present]
                if masked:
                    conditions += [] if needed is None else [needed]
                    conditions += [wide_t] if present is not None else []
                queries = [(i, t) for i in query_places for t in times]
                keys = [(f, r, c) for f in frames for r, c in key_places]
                first = present is None and needed is None

                def all_queries(queries=queries, keys=keys, first=first):
                    for start in range(0, len(queries), 2):
                        add(queries[start : start + 2], keys, masked, first)

                if conditions:
                    pl.when(functools.reduce(lambda a, b: a & b, conditions))(all_queries)
                else:
                    all_queries()

    pl.when(everything)(lambda: run(False))
    pl.when(jnp.logical_not(everything))(lambda: run(True))
    for i, (r, c) in enumerate(places):
        for t in (0, 1):
            both = sums[i * 2 + t]
            out_ref[(t * 4 + r) * 4 + c] = (both[:, :TILE] / both[:, TILE:]).astype(BF16)


def attend(slab, last_slab, windows, q, kv, low, high):
    def whole(array):
        return pl.BlockSpec(array.shape, lambda i, j: (0,) * array.ndim)

    smem = pl.BlockSpec(memory_space=pltpu.SMEM)
    return pl.pallas_call(
        functools.partial(attend_kernel, last_slab=last_slab),
        grid=(2, 2),
        in_specs=[smem, smem] + [whole(x) for x in (q, kv, low, high)],
        out_specs=whole(q),
        out_shape=jax.ShapeDtypeStruct(q.shape, BF16),
        scratch_shapes=[pltpu.VMEM((8, TILE, 2 * TILE), F32)],
        compiler_params=pltpu.CompilerParams(vmem_limit_bytes=VMEM_LIMIT),
    )(slab, windows, q, kv, low, high)


def on_device(queries, keys, values, q_gain, k_gain, windows):
    slabs = lax.axis_size("slab")
    slab = lax.axis_index("slab").astype(jnp.int32).reshape(1)

    def exchange(array):
        return lax.all_to_all(array, "head", split_axis=0, concat_axis=0, tiled=True)

    kv = exchange(prep_kv(keys, values, k_gain))
    forward = [(i, i + 1) for i in range(slabs - 1)]
    backward = [(b, a) for a, b in forward]
    low = lax.ppermute(kv[16:], "slab", forward)
    high = lax.ppermute(kv[:16], "slab", backward)
    q = exchange(prep_q(queries, q_gain))
    result = attend(slab, slabs - 1, windows, q, kv, low, high)
    return merge_heads(exchange(result))


def solution(mesh):
    rows = P(("slab", "head"), None)
    return jax.shard_map(
        on_device,
        mesh=mesh,
        in_specs=(rows, rows, rows, P(), P(), P("head", None)),
        out_specs=rows,
        check_vma=False,
    )
```

profile of v0, /device:TPU:10, one launch (start us, length us, event | category | flops | bytes accessed | tf_op | source)
XLA Modules:
  0.0 155.3 jit_solution(9627587220548996059)
XLA Ops:
  0.0 6.3 %shard_map.65 = bf16[32,2,128,128]{3,2,1,0:T(8,128)(2,1)} custom-call(bf16[128,4096]{1,0:T(8,128)(2,1)} %keys_ref.1, bf16[128,4096]{1,0:T(8,128)(2,1)} %values_ref.1, f32[1,128]{1,0:T(1,128)} %bitcast.3), custom_call_target="tpu_custom_call" | custom-call | tf_op jit(solution)/shard_map/pallas_call | solution.py:47
  6.3 11.6 %all-to-all-start.1 = ((bf16[32,2,128,128]{3,2,1,0:T(8,128)(2,1)}), bf16[32,2,128,128]{3,2,1,0:T(8,128)(2,1)S(1)}, u32[]{:S(2)}, u32[]{:S(2)}) async-start(bf16[32,2,128,128]{3,2,1,0:T(8,128)(2,1)} %shard_map.65), calls=%async_computation.1 | async-start | bytes 4194304 | tf_op jit(solution)/shard_map/all_to_all | solution.py:198
  17.9 5.7 %shard_map.64 = bf16[32,128,128]{2,1,0:T(8,128)(2,1)} custom-call(bf16[128,4096]{1,0:T(8,128)(2,1)} %queries_ref.1, f32[1,128]{1,0:T(1,128)} %bitcast.4), custom_call_target="tpu_custom_call" | custom-call | tf_op jit(solution)/shard_map/pallas_call | solution.py:58
  23.7 43.5 %all-to-all-done.1.kv_ref = bf16[32,2,128,128]{3,2,1,0:T(8,128)(2,1)S(1)} async-done(((bf16[32,2,128,128]{3,2,1,0:T(8,128)(2,1)}), bf16[32,2,128,128]{3,2,1,0:T(8,128)(2,1)S(1)}, u32[]{:S(2)}, u32[]{:S(2)}) %all-to-all-start.1) | async-done | bytes 2097184 | tf_op jit(solution)/shard_map/all_to_all | solution.py:198
  67.2 0.0 copy-start.1
  67.2 6.9 %all-to-all-start = ((bf16[32,128,128]{2,1,0:T(8,128)(2,1)}), bf16[32,128,128]{2,1,0:T(8,128)(2,1)S(1)}, u32[]{:S(2)}, u32[]{:S(2)}) async-start(bf16[32,128,128]{2,1,0:T(8,128)(2,1)} %shard_map.64), calls=%async_computation | async-start | bytes 2097152 | tf_op jit(solution)/shard_map/all_to_all | solution.py:198
  74.0 0.0 copy-start
  74.1 1.4 fusion
  75.5 0.0 copy-done.1
  75.5 1.9 %collective-permute-start = (bf16[16,2,128,128]{3,2,1,0:T(8,128)(2,1)}, bf16[16,2,128,128]{3,2,1,0:T(8,128)(2,1)S(1)}, u32[]{:S(2)}, u32[]{:S(2)}) collective-permute-start(bf16[16,2,128,128]{3,2,1,0:T(8,128)(2,1)} %get-tuple-element.6), channel_id=1, source_target_pairs={{0,32},{32,64},{64,96},{96,128},{128,160},{160,192},{192,224},{1,3... | collective-permute-start | bytes 3145736 | tf_op jit(solution)/shard_map/ppermute | solution.py:203
  77.4 3.6 %collective-permute-start.1 = (bf16[16,2,128,128]{3,2,1,0:T(8,128)(2,1)}, bf16[16,2,128,128]{3,2,1,0:T(8,128)(2,1)S(1)}, u32[]{:S(2)}, u32[]{:S(2)}) collective-permute-start(bf16[16,2,128,128]{3,2,1,0:T(8,128)(2,1)} %get-tuple-element.5), channel_id=1, source_target_pairs={{32,0},{64,32},{96,64},{128,96},{160,128},{192,160},{224,192},{33,... | collective-permute-start | bytes 3145736 | tf_op jit(solution)/shard_map/ppermute | solution.py:204
  81.1 20.0 %all-to-all-done.q_ref = bf16[32,128,128]{2,1,0:T(8,128)(2,1)S(1)} async-done(((bf16[32,128,128]{2,1,0:T(8,128)(2,1)}), bf16[32,128,128]{2,1,0:T(8,128)(2,1)S(1)}, u32[]{:S(2)}, u32[]{:S(2)}) %all-to-all-start) | async-done | bytes 1048608 | tf_op jit(solution)/shard_map/all_to_all | solution.py:198
  101.1 0.0 collective-permute-done.low_ref
  101.1 0.0 collective-permute-done.1.high_ref
  101.1 0.0 copy-done
  101.1 16.5 %shard_map.66 = bf16[32,128,128]{2,1,0:T(8,128)(2,1)S(1)} custom-call(s32[1]{0:T(128)} %bitcast.slab_ref, s32[1,3]{1,0:T(1,128)S(1)} %copy-done, bf16[32,128,128]{2,1,0:T(8,128)(2,1)S(1)} %all-to-all-done.q_ref, bf16[32,2,128,128]{3,2,1,0:T(8,128)(2,1)} %copy-done.1, bf16[16,2,128,128]{3,2,1,0:T(8,128)(2,1)S(1)} %collective-permute-done.low_ref, ...), custom_call_target="tpu_custom_call" | custom-call | tf_op jit(solution)/shard_map/pallas_call | solution.py:182
  117.6 32.5 %all_to_all.15.heads_ref = bf16[32,128,128]{2,1,0:T(8,128)(2,1)} all-to-all(bf16[32,128,128]{2,1,0:T(8,128)(2,1)S(1)} %shard_map.66), channel_id=1, replica_groups=mesh['slab'=8,'head'=32] {'head'}, dimensions={0} | all-to-all | bytes 2097152 | tf_op jit(solution)/shard_map/all_to_all | solution.py:198
  150.1 5.2 %shard_map.67 = bf16[128,4096]{1,0:T(8,128)(2,1)} custom-call(bf16[32,128,128]{2,1,0:T(8,128)(2,1)} %all_to_all.15.heads_ref), custom_call_target="tpu_custom_call" | custom-call | tf_op jit(solution)/shard_map/pallas_call | solution.py:72
Async XLA Ops:
  6.3 60.9 %all-to-all-start.1 = ((bf16[32,2,128,128]{3,2,1,0:T(8,128)(2,1)}), bf16[32,2,128,128]{3,2,1,0:T(8,128)(2,1)S(1)}, u32[]{:S(2)}, u32[]{:S(2)}) async-start(bf16[32,2,128,128]{3,2,1,0:T(8,128)(2,1)} %shard_map.65), calls=%async_computation.1 | async-start | bytes 4194304 | tf_op jit(solution)/shard_map/all_to_all | solution.py:198
  67.2 8.3 %copy-start.1 = (bf16[32,2,128,128]{3,2,1,0:T(8,128)(2,1)}, bf16[32,2,128,128]{3,2,1,0:T(8,128)(2,1)S(1)}, u32[]{:S(2)}) copy-start(bf16[32,2,128,128]{3,2,1,0:T(8,128)(2,1)S(1)} %all-to-all-done.1.kv_ref) | copy-start | bytes 6291460
  67.2 33.9 %all-to-all-start = ((bf16[32,128,128]{2,1,0:T(8,128)(2,1)}), bf16[32,128,128]{2,1,0:T(8,128)(2,1)S(1)}, u32[]{:S(2)}, u32[]{:S(2)}) async-start(bf16[32,128,128]{2,1,0:T(8,128)(2,1)} %shard_map.64), calls=%async_computation | async-start | bytes 2097152 | tf_op jit(solution)/shard_map/all_to_all | solution.py:198
  74.0 27.1 %copy-start = (s32[1,3]{1,0:T(1,128)S(1)}, s32[1,3]{1,0:T(1,128)}, u32[]{:S(2)}) copy-start(s32[1,3]{1,0:T(1,128)} %windows_ref.1) | copy-start | bytes 40
  75.5 25.6 %collective-permute-start = (bf16[16,2,128,128]{3,2,1,0:T(8,128)(2,1)}, bf16[16,2,128,128]{3,2,1,0:T(8,128)(2,1)S(1)}, u32[]{:S(2)}, u32[]{:S(2)}) collective-permute-start(bf16[16,2,128,128]{3,2,1,0:T(8,128)(2,1)} %get-tuple-element.6), channel_id=1, source_target_pairs={{0,32},{32,64},{64,96},{96,128},{128,160},{160,192},{192,224},{1,3... | collective-permute-start | bytes 3145736 | tf_op jit(solution)/shard_map/ppermute | solution.py:203
  77.4 23.7 %collective-permute-start.1 = (bf16[16,2,128,128]{3,2,1,0:T(8,128)(2,1)}, bf16[16,2,128,128]{3,2,1,0:T(8,128)(2,1)S(1)}, u32[]{:S(2)}, u32[]{:S(2)}) collective-permute-start(bf16[16,2,128,128]{3,2,1,0:T(8,128)(2,1)} %get-tuple-element.5), channel_id=1, source_target_pairs={{32,0},{64,32},{96,64},{128,96},{160,128},{192,160},{224,192},{33,... | collective-permute-start | bytes 3145736 | tf_op jit(solution)/shard_map/ppermute | solution.py:204
where the time goes:
time: 157 us; the launch traced here: 155 us
  waiting for transfers between devices  63.5 us (40%)
  Pallas kernels  33.8 us (22%)
  blocking collectives  32.5 us (21%)
  starting transfers between devices  24 us (15%)
    all_to_all x2, waiting for transfers between devices, exchange(): lax.all_to_all(array, 'head', split_axis=0, concat_axis=0, tiled=True)  63.5 us
    all_to_all x1, blocking collectives, exchange(): lax.all_to_all(array, 'head', split_axis=0, concat_axis=0, tiled=True)  32.5 us
    all_to_all x2, starting transfers between devices, exchange(): lax.all_to_all(array, 'head', split_axis=0, concat_axis=0, tiled=True)  18.5 us
    pallas_call x1, Pallas kernels, attend(): pl.pallas_call(functools.partial(attend_kernel, last_slab=last_slab), gri...  16.5 us
    pallas_call x1, Pallas kernels, prep_kv(): pl.pallas_call(prep_kv_kernel, grid=(steps,), in_specs=[wide, wide, pl.Bl...  6.31 us
    pallas_call x1, Pallas kernels, prep_q(): pl.pallas_call(prep_q_kernel, grid=(steps,), in_specs=[pl.BlockSpec((TILE...  5.73 us
    pallas_call x1, Pallas kernels, merge_heads(): pl.pallas_call(merge_kernel, grid=(steps,), in_specs=[pl.BlockSpec((HEADS...  5.22 us
    ppermute x1, starting transfers between devices, on_device(): high = lax.ppermute(kv[:16], 'slab', backward)  3.64 us
  transfers between devices with their start and end apart: 4, of which 2 were waited for; matrix products, arithmetic and copies ran while one was open for 1% of the time, Pallas kernels for 4%

commit v1 on v0

v1 whole, which is shorter than its diff:
```python
import functools
import math

import jax
import jax.numpy as jnp
from jax import lax
from jax.experimental import pallas as pl
from jax.experimental.pallas import tpu as pltpu
from jax.sharding import PartitionSpec as P

TILE = 128
ROWS = 4
FRAME = 16
PREP_HEADS = 16
PREP_VMEM = 60 * 2**20
SMALL_VMEM = 16 * 2**20
ATTEND_VMEM = 16 * 2**20
EXP2_SCALE = math.log2(math.e) / math.sqrt(TILE)
F32 = jnp.float32
BF16 = jnp.bfloat16
KEY, VALUE = 0, 1


def normed(block, gain):
    widened = block.astype(F32)
    mean_sq = jnp.mean(widened * widened, axis=-1, keepdims=True)
    return (widened * lax.rsqrt(mean_sq + 1e-06) * gain).astype(BF16)


def prep_kernel(queries_ref, keys_ref, values_ref, q_gain_ref, k_gain_ref, q_ref, kv_ref):
    q_gain, k_gain = q_gain_ref[...], k_gain_ref[...]
    for index in range(PREP_HEADS):
        columns = slice(index * TILE, (index + 1) * TILE)
        kv_ref[index, KEY] = normed(keys_ref[:, columns], k_gain)
        kv_ref[index, VALUE] = values_ref[:, columns]
        q_ref[index] = normed(queries_ref[:, columns], q_gain)


def prep(queries, keys, values, q_gain, k_gain):
    steps = keys.shape[1] // (TILE * PREP_HEADS)
    heads = steps * PREP_HEADS
    wide = pl.BlockSpec((TILE, TILE * PREP_HEADS), lambda i: (0, i))
    gain = pl.BlockSpec((1, TILE), lambda i: (0, 0))
    return pl.pallas_call(
        prep_kernel,
        grid=(steps,),
        in_specs=[wide, wide, wide, gain, gain],
        out_specs=[
            pl.BlockSpec((PREP_HEADS, TILE, TILE), lambda i: (i, 0, 0)),
            pl.BlockSpec((PREP_HEADS, 2, TILE, TILE), lambda i: (i, 0, 0, 0)),
        ],
        out_shape=[
            jax.ShapeDtypeStruct((heads, TILE, TILE), BF16),
            jax.ShapeDtypeStruct((heads, 2, TILE, TILE), BF16),
        ],
        compiler_params=pltpu.CompilerParams(vmem_limit_bytes=PREP_VMEM),
    )(queries, keys, values, q_gain.reshape(1, TILE), k_gain.reshape(1, TILE))


def merge_kernel(heads_ref, out_ref):
    for index in range(PREP_HEADS):
        out_ref[:, index * TILE : (index + 1) * TILE] = heads_ref[index]


def merge_heads(heads):
    steps = heads.shape[0] // PREP_HEADS
    return pl.pallas_call(
        merge_kernel,
        grid=(steps,),
        in_specs=[pl.BlockSpec((PREP_HEADS, TILE, TILE), lambda i: (i, 0, 0))],
        out_specs=pl.BlockSpec((TILE, TILE * PREP_HEADS), lambda i: (0, i)),
        out_shape=jax.ShapeDtypeStruct((TILE, heads.shape[0] * TILE), BF16),
        compiler_params=pltpu.CompilerParams(vmem_limit_bytes=SMALL_VMEM),
    )(heads)


def stack(blocks):
    return blocks[0] if len(blocks) == 1 else jnp.concatenate(blocks, axis=0)


def quarter(step, wide_r, wide_c):
    half_r, half_c = step // 2, step % 2
    outer_r, inner_r, extra_r, first_r = 3 * half_r, 1 + half_r, 2 - half_r, 2 * half_r
    outer_c, inner_c, extra_c, first_c = 3 * half_c, 1 + half_c, 2 - half_c, 2 * half_c
    places = [(outer_r, outer_c), (outer_r, inner_c), (inner_r, outer_c), (inner_r, inner_c)]
    shared_r, shared_c = (first_r, first_r + 1), (first_c, first_c + 1)
    groups = [
        ([0, 1, 2, 3], [(r, c) for r in shared_r for c in shared_c], None),
        ([1, 3], [(r, extra_c) for r in shared_r], wide_c),
        ([2, 3], [(extra_r, c) for c in shared_c], wide_r),
        ([3], [(extra_r, extra_c)], wide_r & wide_c),
    ]
    return places, groups


def weighted_sums(q, keys, values, ones, biases):
    total = None
    for start in range(0, len(keys), 2):
        k = stack(keys[start : start + 2])
        v = stack(values[start : start + 2])
        scores = lax.dot_general(q, k, (((1,), (1,)), ((), ())), preferred_element_type=F32)
        if biases is not None:
            scores = scores + stack(
                [
                    jnp.concatenate(
                        [jnp.full((TILE, TILE), b, F32) for b in row[start : start + 2]], axis=1
                    )
                    for row in biases
                ]
            )
        weights = jnp.exp2(scores * EXP2_SCALE).astype(BF16)
        widened = jnp.concatenate([v, jnp.full(v.shape, ones, BF16)], axis=1)
        part = jnp.dot(weights, widened, preferred_element_type=F32)
        total = part if total is None else total + part
    return total


def outside(conditions):
    inside = functools.reduce(lambda a, b: a & b, conditions)
    return jnp.where(inside, 0.0, -1e30).astype(F32)


def run_groups(groups, add):
    for query_places, key_places, needed in groups:
        action = functools.partial(add, query_places, key_places, needed is None)
        if needed is not None:
            pl.when(needed)(action)
        else:
            action()


def near_tiles(r, c):
    return [
        (a, b)
        for a in range(max(r - 1, 0), min(r + 2, ROWS))
        for b in range(max(c - 1, 0), min(c + 2, ROWS))
    ]


def own_kernel(windows_ref, q_ref, kv_ref, sums_ref):
    wide_t, wide_r, wide_c = (windows_ref[0, axis] >= 1 for axis in range(3))
    everything = wide_t & wide_r & wide_c

    def tile(t, place):
        return t * FRAME + place[0] * ROWS + place[1]

    def sums_of(place, keys, biases):
        return weighted_sums(
            stack([q_ref[tile(t, place)] for t in (0, 1)]),
            [kv_ref[tile(t, key), KEY] for t, key in keys],
            [kv_ref[tile(t, key), VALUE] for t, key in keys],
            1.0,
            biases,
        )

    def step(index, carry):
        places, groups = quarter(index, wide_r, wide_c)

        def add(query_places, key_places, first):
            keys = [(t, place) for t in (0, 1) for place in key_places]
            for i in query_places:
                r, c = places[i]
                biases = [
                    [
                        outside([wide_t | (t == u), wide_r | (r == kr), wide_c | (c == kc)])
                        for u, (kr, kc) in keys
                    ]
                    for t in (0, 1)
                ]
                total = sums_of(places[i], keys, biases)
                for t in (0, 1):
                    rows = total[t * TILE : (t + 1) * TILE]
                    at = tile(t, places[i])
                    if first:
                        sums_ref[at] = rows
                    else:
                        sums_ref[at] += rows

        run_groups(groups, add)
        return carry

    @pl.when(everything)
    def _():
        for r in range(ROWS):
            for c in range(ROWS):
                total = sums_of((r, c), [(t, key) for t in (0, 1) for key in near_tiles(r, c)], None)
                for t in (0, 1):
                    sums_ref[tile(t, (r, c))] = total[t * TILE : (t + 1) * TILE]

    @pl.when(jnp.logical_not(everything))
    def _():
        lax.fori_loop(0, 4, step, 0)


def halo_kernel(place_ref, windows_ref, q_ref, halo_ref, sums_ref, base_ref, out_ref, acc):
    del base_ref
    start = place_ref[0] * FRAME
    wide_t, wide_r, wide_c = (windows_ref[0, axis] >= 1 for axis in range(3))
    everything = wide_t & wide_r & wide_c
    ones = place_ref[1].astype(F32).astype(BF16)

    def finish(at, both):
        out_ref[at] = (both[:, :TILE] / both[:, TILE:]).astype(BF16)

    def sums_of(ats, key_places, biases):
        return weighted_sums(
            stack([q_ref[at] for at in ats]),
            [halo_ref[r * ROWS + c, KEY] for r, c in key_places],
            [halo_ref[r * ROWS + c, VALUE] for r, c in key_places],
            ones,
            biases,
        )

    def step(index, carry):
        places, groups = quarter(index, wide_r, wide_c)
        ats = [start + r * ROWS + c for r, c in places]
        for i in range(4):
            acc[i] = sums_ref[ats[i]]

        def add(query_places, key_places, first):
            for begin in range(0, len(query_places), 2):
                chosen = query_places[begin : begin + 2]
                biases = [
                    [
                        outside([wide_r | (places[i][0] == r), wide_c | (places[i][1] == c)])
                        for r, c in key_places
                    ]
                    for i in chosen
                ]
                total = sums_of([ats[i] for i in chosen], key_places, biases)
                for n, i in enumerate(chosen):
                    acc[i] += total[n * TILE : (n + 1) * TILE]

        run_groups(groups, add)
        for i in range(4):
            finish(ats[i], acc[i])
        return carry

    @pl.when(everything)
    def _():
        for r in range(ROWS):
            for c in range(ROWS):
                at = start + r * ROWS + c
                finish(at, sums_ref[at] + sums_of([at], near_tiles(r, c), None))

    @pl.when(wide_t & jnp.logical_not(everything))
    def _():
        lax.fori_loop(0, 4, step, 0)

    @pl.when(jnp.logical_not(wide_t))
    def _():
        for index in range(FRAME):
            finish(start + index, sums_ref[start + index])


SMEM_SPEC = pl.BlockSpec(memory_space=pltpu.SMEM)
VMEM_SPEC = pl.BlockSpec(memory_space=pltpu.VMEM)


def attend_own(windows, q, kv):
    return pl.pallas_call(
        own_kernel,
        in_specs=[SMEM_SPEC, VMEM_SPEC, VMEM_SPEC],
        out_specs=VMEM_SPEC,
        out_shape=jax.ShapeDtypeStruct((q.shape[0], TILE, 2 * TILE), F32),
        compiler_params=pltpu.CompilerParams(vmem_limit_bytes=ATTEND_VMEM),
        cost_estimate=pl.CostEstimate(
            flops=400 * 6 * TILE**3, bytes_accessed=2**23, transcendentals=400 * TILE**2
        ),
    )(windows, q, kv)


def attend_halo(place, windows, q, halo, sums, base):
    return pl.pallas_call(
        halo_kernel,
        in_specs=[SMEM_SPEC, SMEM_SPEC] + [VMEM_SPEC] * 4,
        out_specs=VMEM_SPEC,
        out_shape=jax.ShapeDtypeStruct(q.shape, BF16),
        input_output_aliases={5: 0},
        scratch_shapes=[pltpu.VMEM((4, TILE, 2 * TILE), F32)],
        compiler_params=pltpu.CompilerParams(vmem_limit_bytes=ATTEND_VMEM),
        cost_estimate=pl.CostEstimate(
            flops=100 * 6 * TILE**3, bytes_accessed=2**22, transcendentals=100 * TILE**2
        ),
    )(place, windows, q, halo, sums, base)


def on_device(queries, keys, values, q_gain, k_gain, windows):
    slabs = lax.axis_size("slab")
    slab = lax.axis_index("slab").astype(jnp.int32)
    odd = slab % 2

    def exchange(array):
        return lax.all_to_all(array, "head", split_axis=0, concat_axis=0, tiled=True)

    q, kv = prep(queries, keys, values, q_gain, k_gain)
    def together(kv):
        return exchange(kv)

    def apart(kv):
        return jnp.stack([exchange(kv[:, KEY]), exchange(kv[:, VALUE])], axis=1)

    kv = lax.cond(odd == 0, together, apart, kv)
    q = exchange(q)

    def frame_of(index):
        return lax.dynamic_slice(kv, (index * FRAME, 0, 0, 0), (FRAME, 2, TILE, TILE))

    def swap(block, low, high):
        pairs = [(a, a + 1) for a in range(low, high, 2)]
        return lax.ppermute(block, "slab", pairs + [(b, a) for a, b in pairs])

    far = swap(frame_of(odd), 1, slabs - 1)
    near = swap(frame_of(1 - odd), 0, slabs)
    far_present = ((slab > 0) & (slab < slabs - 1)).astype(jnp.int32)
    sums = attend_own(windows, q, kv)
    result = jnp.zeros(q.shape, BF16)
    result = attend_halo(jnp.stack([1 - odd, 1]), windows, q, near, sums, result)
    result = attend_halo(jnp.stack([odd, far_present]), windows, q, far, sums, result)
    return merge_heads(exchange(result))


def solution(mesh):
    rows = P(("slab", "head"), None)
    return jax.shard_map(
        on_device,
        mesh=mesh,
        in_specs=(rows, rows, rows, P(), P(), P("head", None)),
        out_specs=rows,
        check_vma=False,
    )
```

time: 157 us -> 137 us (0.87)
  the two profiles are of different devices: /device:TPU:10 before, /device:TPU:19 now
where the time goes in v1:
time: 137 us; the launch traced here: 136 us
  blocking collectives  91.3 us (67%)
  Pallas kernels  19.3 us (14%)
  waiting for transfers between devices  13.2 us (10%)
  starting transfers between devices  8.29 us (6%)
  local copies, waits for them, and re-layouts  3.52 us (3%)
    all_to_all x3, blocking collectives, exchange(): lax.all_to_all(array, 'head', split_axis=0, concat_axis=0, tiled=True)  91.3 us
    all_to_all x1, waiting for transfers between devices, exchange(): lax.all_to_all(array, 'head', split_axis=0, concat_axis=0, tiled=True)  13.2 us
    pallas_call x1, Pallas kernels, attend_own(): pl.pallas_call(own_kernel, in_specs=[SMEM_SPEC, VMEM_SPEC, VMEM_SPEC], ou...  8.97 us
    pallas_call x2, Pallas kernels, attend_halo(): pl.pallas_call(halo_kernel, in_specs=[SMEM_SPEC, SMEM_SPEC] + [VMEM_SPEC]...  5.34 us
    all_to_all x1, starting transfers between devices, exchange(): lax.all_to_all(array, 'head', split_axis=0, concat_axis=0, tiled=True)  4.99 us
    pallas_call x1, Pallas kernels, prep(): pl.pallas_call(prep_kernel, grid=(steps,), in_specs=[wide, wide, wide, ga...  3.88 us
    ppermute x2, starting transfers between devices, swap(): return lax.ppermute(block, 'slab', pairs + [(b, a) for a, b in pairs])  3.29 us
  transfers between devices with their start and end apart: 3, of which 1 were waited for; matrix products, arithmetic and copies ran while one was open for 1% of the time, Pallas kernels for 9%

profile of v1, /device:TPU:19, one launch (start us, length us, event | category | flops | bytes accessed | tf_op | source)
XLA Modules:
  0.0 136.1 jit_solution(14703886571166195303)
XLA Ops:
  0.0 3.9 %shard_map.64 = (bf16[32,128,128]{2,1,0:T(8,128)(2,1)}, bf16[32,2,128,128]{3,2,1,0:T(8,128)(2,1)}) custom-call(bf16[128,4096]{1,0:T(8,128)(2,1)} %queries_ref.1, bf16[128,4096]{1,0:T(8,128)(2,1)} %keys_ref.1, bf16[128,4096]{1,0:T(8,128)(2,1)} %values_ref.1, f32[1,128]{1,0:T(1,128)} %bitcast.17, f32[1,128]{1,0:T(1,128)} %bitcast.18), custom_call_target="tpu_custom_call" | custom-call | tf_op jit(solution)/shard_map/pallas_call | solution.py:44
  3.9 64.2 %conditional.1 = (bf16[32,2,128,128]{3,2,1,0:T(8,128)(2,1)S(1)}) conditional(s32[]{:T(128)} %convert_element_type.4, bf16[32,2,128,128]{3,2,1,0:T(8,128)(2,1)} %get-tuple-element.13, bf16[32,2,128,128]{3,2,1,0:T(8,128)(2,1)} %get-tuple-element.13), branch_computations={%region_0.1_spmd, %region_1.2_spmd} | conditional | flops 1048576 | bytes 16777224 | solution.py:303
  3.9 1.7 %slice_bitcast_fusion.1 = (bf16[32,128,128]{2,1,0:T(8,128)(2,1)S(1)}, bf16[32,128,128]{2,1,0:T(8,128)(2,1)S(1)}) fusion(bf16[32,2,128,128]{3,2,1,0:T(8,128)(2,1)} %param), kind=kLoop, calls=%fused_computation.2 | loop fusion | bytes 4194304 | tf_op jit(solution)/shard_map/cond/branch_0_fun/squeeze | solution.py:301
  5.6 39.1 %all_to_all.22 = bf16[32,128,128]{2,1,0:T(8,128)(2,1)S(1)} all-to-all(bf16[32,128,128]{2,1,0:T(8,128)(2,1)S(1)} %get-tuple-element.16), channel_id=1, replica_groups=mesh['slab'=8,'head'=32] {'head'}, dimensions={0} | all-to-all | bytes 2097152 | tf_op jit(solution)/shard_map/cond/branch_0_fun/all_to_all | solution.py:294
  44.7 23.1 %all_to_all.23 = bf16[32,128,128]{2,1,0:T(8,128)(2,1)S(1)} all-to-all(bf16[32,128,128]{2,1,0:T(8,128)(2,1)S(1)} %get-tuple-element.15), channel_id=1, replica_groups=mesh['slab'=8,'head'=32] {'head'}, dimensions={0} | all-to-all | bytes 2097152 | tf_op jit(solution)/shard_map/cond/branch_0_fun/all_to_all | solution.py:294
  67.7 0.2 pad_maximum_fusion
  67.9 0.1 copy.21
  68.1 0.0 copy-start.1
  68.1 5.0 %all-to-all-start.3 = ((bf16[32,128,128]{2,1,0:T(8,128)(2,1)}), bf16[32,128,128]{2,1,0:T(8,128)(2,1)S(1)}, u32[]{:S(2)}, u32[]{:S(2)}) async-start(bf16[32,128,128]{2,1,0:T(8,128)(2,1)} %get-tuple-element.12), calls=%async_computation.3 | async-start | bytes 2097152 | tf_op jit(solution)/shard_map/all_to_all | solution.py:294
  73.1 0.0 copy-start
  73.1 1.5 %constant_dynamic-slice_fusion = (bf16[16,2,128,128]{3,2,1,0:T(8,128)(2,1)}, bf16[16,2,128,128]{3,2,1,0:T(8,128)(2,1)}) fusion(bf16[32,2,128,128]{3,2,1,0:T(8,128)(2,1)S(1)} %get-tuple-element.14.kv_ref, s32[]{:T(128)S(6)} %select_n.15, s32[]{:T(128)S(6)} %select_n.14), kind=kLoop, calls=%fused_computation.5 | loop fusion | bytes 4194312 | tf_op jit(solution)/shard_map/dynamic_slice | solution.py:307
  74.6 0.0 copy-done.1
  74.6 0.0 collective-permute-start.1
  74.6 3.3 %collective-permute-start = (bf16[16,2,128,128]{3,2,1,0:T(8,128)(2,1)}, bf16[16,2,128,128]{3,2,1,0:T(8,128)(2,1)S(1)}, u32[]{:S(2)}, u32[]{:S(2)}) collective-permute-start(bf16[16,2,128,128]{3,2,1,0:T(8,128)(2,1)} %get-tuple-element.18), channel_id=1, source_target_pairs={{32,64},{96,128},{160,192},{64,32},{128,96},{192,160},{33,65},{97,... | collective-permute-start | bytes 3145736 | tf_op jit(solution)/shard_map/ppermute | solution.py:311
  77.9 0.1 pad_add_fusion.place_ref
  78.0 0.1 pad_add_fusion.1.place_ref
  78.1 13.2 %all-to-all-done.3.q_ref = bf16[32,128,128]{2,1,0:T(8,128)(2,1)S(1)} async-done(((bf16[32,128,128]{2,1,0:T(8,128)(2,1)}), bf16[32,128,128]{2,1,0:T(8,128)(2,1)S(1)}, u32[]{:S(2)}, u32[]{:S(2)}) %all-to-all-start.3) | async-done | bytes 1048608 | tf_op jit(solution)/shard_map/all_to_all | solution.py:294
  91.3 0.0 copy-done
  91.3 9.0 %shard_map.65.sums_ref = f32[32,128,256]{2,1,0:T(8,128)S(1)} custom-call(s32[1,3]{1,0:T(1,128)S(1)} %copy-done, bf16[32,128,128]{2,1,0:T(8,128)(2,1)S(1)} %all-to-all-done.3.q_ref, bf16[32,2,128,128]{3,2,1,0:T(8,128)(2,1)} %copy-done.1), custom_call_target="tpu_custom_call" | custom-call | flops 5033164800 | bytes 8388608 | tf_op jit(solution)/shard_map/pallas_call | solution.py:261
  100.2 0.0 collective-permute-done.1.halo_ref
  100.2 0.2 broadcast_in_dim.3.base_ref
  100.5 2.7 %shard_map.66.base_ref = bf16[32,128,128]{2,1,0:T(8,128)(2,1)S(1)} custom-call(s32[2]{0:T(128)S(1)} %pad_add_fusion.1.place_ref, s32[1,3]{1,0:T(1,128)S(1)} %copy-done, bf16[32,128,128]{2,1,0:T(8,128)(2,1)S(1)} %all-to-all-done.3.q_ref, bf16[16,2,128,128]{3,2,1,0:T(8,128)(2,1)S(1)} %collective-permute-done.1.halo_ref, ...), custom_call_target="tpu_custom_call", output_to_operand_aliasing={{}: (5, {})} | custom-call | flops 1258291200 | bytes 4194304 | tf_op jit(solution)/shard_map/pallas_call | solution.py:274
  103.2 0.0 collective-permute-done.halo_ref
  103.2 2.7 %shard_map.67 = bf16[32,128,128]{2,1,0:T(8,128)(2,1)S(1)} custom-call(s32[2]{0:T(128)S(1)} %pad_add_fusion.place_ref, s32[1,3]{1,0:T(1,128)S(1)} %copy-done, bf16[32,128,128]{2,1,0:T(8,128)(2,1)S(1)} %all-to-all-done.3.q_ref, bf16[16,2,128,128]{3,2,1,0:T(8,128)(2,1)S(1)} %collective-permute-done.halo_ref, ...), custom_call_target="tpu_custom_call", output_to_operand_aliasing={{}: (5, {})} | custom-call | flops 1258291200 | bytes 4194304 | tf_op jit(solution)/shard_map/pallas_call | solution.py:274
  105.8 29.2 %all_to_all.25.heads_ref = bf16[32,128,128]{2,1,0:T(8,128)(2,1)S(1)} all-to-all(bf16[32,128,128]{2,1,0:T(8,128)(2,1)S(1)} %shard_map.67), channel_id=1, replica_groups=mesh['slab'=8,'head'=32] {'head'}, dimensions={0} | all-to-all | bytes 2097152 | tf_op jit(solution)/shard_map/all_to_all | solution.py:294
  135.0 1.1 shard_map.68
Async XLA Ops:
  68.1 6.5 %copy-start.1 = (bf16[32,2,128,128]{3,2,1,0:T(8,128)(2,1)}, bf16[32,2,128,128]{3,2,1,0:T(8,128)(2,1)S(1)}, u32[]{:S(2)}) copy-start(bf16[32,2,128,128]{3,2,1,0:T(8,128)(2,1)S(1)} %get-tuple-element.14.kv_ref) | copy-start | bytes 6291460
  68.1 23.1 %all-to-all-start.3 = ((bf16[32,128,128]{2,1,0:T(8,128)(2,1)}), bf16[32,128,128]{2,1,0:T(8,128)(2,1)S(1)}, u32[]{:S(2)}, u32[]{:S(2)}) async-start(bf16[32,128,128]{2,1,0:T(8,128)(2,1)} %get-tuple-element.12), calls=%async_computation.3 | async-start | bytes 2097152 | tf_op jit(solution)/shard_map/all_to_all | solution.py:294
  73.1 18.1 %copy-start = (s32[1,3]{1,0:T(1,128)S(1)}, s32[1,3]{1,0:T(1,128)}, u32[]{:S(2)}) copy-start(s32[1,3]{1,0:T(1,128)} %windows_ref.5) | copy-start | bytes 40
  74.6 25.6 %collective-permute-start.1 = (bf16[16,2,128,128]{3,2,1,0:T(8,128)(2,1)}, bf16[16,2,128,128]{3,2,1,0:T(8,128)(2,1)S(1)}, u32[]{:S(2)}, u32[]{:S(2)}) collective-permute-start(bf16[16,2,128,128]{3,2,1,0:T(8,128)(2,1)} %get-tuple-element.17), channel_id=1, source_target_pairs={{0,32},{64,96},{128,160},{192,224},{32,0},{96,64},{160,128},{224,1... | collective-permute-start | bytes 3145736 | tf_op jit(solution)/shard_map/ppermute | solution.py:311
  74.6 28.6 %collective-permute-start = (bf16[16,2,128,128]{3,2,1,0:T(8,128)(2,1)}, bf16[16,2,128,128]{3,2,1,0:T(8,128)(2,1)S(1)}, u32[]{:S(2)}, u32[]{:S(2)}) collective-permute-start(bf16[16,2,128,128]{3,2,1,0:T(8,128)(2,1)} %get-tuple-element.18), channel_id=1, source_target_pairs={{32,64},{96,128},{160,192},{64,32},{128,96},{192,160},{33,65},{97,... | collective-permute-start | bytes 3145736 | tf_op jit(solution)/shard_map/ppermute | solution.py:311

commit v2 on v1

v2 whole, which is shorter than its diff:
```python
import functools
import itertools
import math

import jax
import jax.numpy as jnp
from jax import lax
from jax.experimental import pallas as pl
from jax.experimental.pallas import tpu as pltpu
from jax.sharding import PartitionSpec as P

TILE = 128
ROWS = 4
FRAME = 16
PREP_HEADS = 16
PREP_VMEM = 60 * 2**20
SMALL_VMEM = 8 * 2**20
ATTEND_VMEM = 16 * 2**20
EXP2_SCALE = math.log2(math.e) / math.sqrt(TILE)
F32 = jnp.float32
BF16 = jnp.bfloat16
KEY, VALUE = 0, 1
ONE, BOTH = (TILE, TILE), (2, TILE, TILE)
SMEM_SPEC = pl.BlockSpec(memory_space=pltpu.SMEM)
VMEM_SPEC = pl.BlockSpec(memory_space=pltpu.VMEM)
ANY_SPEC = pl.BlockSpec(memory_space=pl.ANY)


def normed(block, gain):
    widened = block.astype(F32)
    mean_sq = jnp.mean(widened * widened, axis=-1, keepdims=True)
    return (widened * lax.rsqrt(mean_sq + 1e-06) * gain).astype(BF16)


def columns(index):
    return slice(index * TILE, (index + 1) * TILE)


def prep_kernel(queries_ref, keys_ref, values_ref, q_gain_ref, k_gain_ref, q_ref, kv_ref):
    q_gain, k_gain = q_gain_ref[...], k_gain_ref[...]
    for index in range(PREP_HEADS):
        block = columns(index)
        kv_ref[index, KEY] = normed(keys_ref[:, block], k_gain)
        kv_ref[index, VALUE] = values_ref[:, block]
        q_ref[index] = normed(queries_ref[:, block], q_gain)


def prep(queries, keys, values, q_gain, k_gain):
    steps = keys.shape[1] // (TILE * PREP_HEADS)
    heads = steps * PREP_HEADS
    wide = pl.BlockSpec((TILE, TILE * PREP_HEADS), lambda i: (0, i))
    gain = pl.BlockSpec((1, TILE), lambda i: (0, 0))
    return pl.pallas_call(
        prep_kernel,
        grid=(steps,),
        in_specs=[wide, wide, wide, gain, gain],
        out_specs=[
            pl.BlockSpec((PREP_HEADS, TILE, TILE), lambda i: (i, 0, 0)),
            pl.BlockSpec((PREP_HEADS, 2, TILE, TILE), lambda i: (i, 0, 0, 0)),
        ],
        out_shape=[
            jax.ShapeDtypeStruct((heads, TILE, TILE), BF16),
            jax.ShapeDtypeStruct((heads, 2, TILE, TILE), BF16),
        ],
        compiler_params=pltpu.CompilerParams(vmem_limit_bytes=PREP_VMEM),
    )(queries, keys, values, q_gain.reshape(1, TILE), k_gain.reshape(1, TILE))


def merge_kernel(heads_ref, out_ref):
    for index in range(PREP_HEADS):
        out_ref[:, columns(index)] = heads_ref[index]


def merge_heads(heads):
    steps = heads.shape[0] // PREP_HEADS
    return pl.pallas_call(
        merge_kernel,
        grid=(steps,),
        in_specs=[pl.BlockSpec((PREP_HEADS, TILE, TILE), lambda i: (i, 0, 0))],
        out_specs=pl.BlockSpec((TILE, TILE * PREP_HEADS), lambda i: (0, i)),
        out_shape=jax.ShapeDtypeStruct((TILE, heads.shape[0] * TILE), BF16),
        compiler_params=pltpu.CompilerParams(vmem_limit_bytes=SMALL_VMEM),
    )(heads)


def stack(blocks):
    return blocks[0] if len(blocks) == 1 else jnp.concatenate(blocks, axis=0)


def weighted_sums(q, keys, values, ones):
    total = None
    for start in range(0, len(keys), 2):
        k = stack(keys[start : start + 2])
        v = stack(values[start : start + 2])
        scores = lax.dot_general(q, k, (((1,), (1,)), ((), ())), preferred_element_type=F32)
        weights = jnp.exp2(scores * EXP2_SCALE).astype(BF16)
        widened = jnp.concatenate([v, jnp.full(v.shape, ones, BF16)], axis=1)
        part = jnp.dot(weights, widened, preferred_element_type=F32)
        total = part if total is None else total + part
    return total


def for_each_window(windows_ref, run):
    for wide in itertools.product((1, 0), repeat=windows_ref.shape[1]):
        same = [(windows_ref[0, axis] >= 1) == bool(w) for axis, w in enumerate(wide)]
        pl.when(functools.reduce(lambda x, y: x & y, same))(functools.partial(run, *wide))


def for_each_place(wide_r, wide_c, straight, visit):
    def near(r, c):
        return [
            a * ROWS + b
            for a in range(max(r - wide_r, 0), min(r + wide_r, ROWS - 1) + 1)
            for b in range(max(c - wide_c, 0), min(c + wide_c, ROWS - 1) + 1)
        ]

    if straight:
        for r, c in itertools.product(range(ROWS), repeat=2):
            visit(r * ROWS + c, near(r, c))
        return

    def reach(half, wide):
        outer, inner = 3 * half, 1 + half
        pair = [2 * half, 2 * half + 1]
        if wide:
            return [(outer, pair), (inner, pair + [2 - half])]
        return [(outer, [outer]), (inner, [inner])]

    def body(index, carry):
        for r, near_r in reach(index // 2, wide_r):
            for c, near_c in reach(index % 2, wide_c):
                visit(r * ROWS + c, [a * ROWS + b for a in near_r for b in near_c])
        return carry

    lax.fori_loop(0, 4, body, 0)


def own_kernel(windows_ref, q_ref, kv_ref, sums_ref):
    def run(wide_t, wide_r, wide_c):
        def visit(place, near_places):
            for times in ((0, 1),) if wide_t else ((0,), (1,)):
                ats = [t * FRAME + place for t in times]
                near = [t * FRAME + n for t in times for n in near_places]
                total = weighted_sums(
                    stack([q_ref[at] for at in ats]),
                    [kv_ref[at, KEY] for at in near],
                    [kv_ref[at, VALUE] for at in near],
                    1.0,
                )
                for n, at in enumerate(ats):
                    sums_ref[at] = total[n * TILE : (n + 1) * TILE]

        for_each_place(wide_r, wide_c, wide_t and wide_r and wide_c, visit)

    for_each_window(windows_ref, run)


def halo_kernel(place_ref, windows_ref, q_ref, near_ref, far_ref, sums_ref, out_ref):
    halos = (
        (near_ref, place_ref[0] * FRAME, 1.0),
        (far_ref, place_ref[1] * FRAME, place_ref[2].astype(F32).astype(BF16)),
    )

    def run(wide_t, wide_r, wide_c):
        def visit(place, near_places):
            for halo_ref, start, ones in halos:
                both = sums_ref[start + place]
                if wide_t:
                    both = both + weighted_sums(
                        q_ref[start + place],
                        [halo_ref[n, KEY] for n in near_places],
                        [halo_ref[n, VALUE] for n in near_places],
                        ones,
                    )
                out_ref[start + place] = (both[:, :TILE] / both[:, TILE:]).astype(BF16)

        for_each_place(wide_r, wide_c, wide_t and wide_r and wide_c, visit)

    for_each_window(windows_ref, run)


def attend_own(windows, q, kv):
    return pl.pallas_call(
        own_kernel,
        in_specs=[SMEM_SPEC] + [VMEM_SPEC] * 2,
        out_specs=VMEM_SPEC,
        out_shape=jax.ShapeDtypeStruct((q.shape[0], TILE, 2 * TILE), F32),
        compiler_params=pltpu.CompilerParams(vmem_limit_bytes=ATTEND_VMEM),
        cost_estimate=pl.CostEstimate(
            flops=400 * 6 * TILE**3, bytes_accessed=2**23, transcendentals=400 * TILE**2
        ),
    )(windows, q, kv)


def attend_halos(place, windows, q, near, far, sums):
    return pl.pallas_call(
        halo_kernel,
        in_specs=[SMEM_SPEC, SMEM_SPEC] + [VMEM_SPEC] * 4,
        out_specs=VMEM_SPEC,
        out_shape=jax.ShapeDtypeStruct(q.shape, BF16),
        compiler_params=pltpu.CompilerParams(vmem_limit_bytes=ATTEND_VMEM),
        cost_estimate=pl.CostEstimate(
            flops=200 * 6 * TILE**3, bytes_accessed=2**23, transcendentals=200 * TILE**2
        ),
    )(place, windows, q, near, far, sums)


def on_device(queries, keys, values, q_gain, k_gain, windows):
    slabs = lax.axis_size("slab")
    slab = lax.axis_index("slab").astype(jnp.int32)
    odd = slab % 2

    def exchange(array):
        return lax.all_to_all(array, "head", split_axis=0, concat_axis=0, tiled=True)

    def together(kv):
        return exchange(kv)

    def apart(kv):
        v = exchange(kv[:, VALUE])
        k = exchange(kv[:, KEY])
        return jnp.stack([k, v], axis=1)

    q, kv = prep(queries, keys, values, q_gain, k_gain)
    kv = lax.cond(odd == 0, together, apart, kv)
    q = exchange(q)

    def frame_of(index):
        return lax.dynamic_slice_in_dim(kv, index * FRAME, FRAME)

    def swap(block, low, high):
        pairs = [(a, a + 1) for a in range(low, high, 2)]
        return lax.ppermute(block, "slab", pairs + [(b, a) for a, b in pairs])

    far = swap(frame_of(odd), 1, slabs - 1)
    near = swap(frame_of(1 - odd), 0, slabs)
    far_present = ((slab > 0) & (slab < slabs - 1)).astype(jnp.int32)
    sums = attend_own(windows, q, kv)
    place = jnp.stack([1 - odd, odd, far_present])
    return merge_heads(exchange(attend_halos(place, windows, q, near, far, sums)))


def solution(mesh):
    rows = P(("slab", "head"), None)
    return jax.shard_map(
        on_device,
        mesh=mesh,
        in_specs=(rows, rows, rows, P(), P(), P("head", None)),
        out_specs=rows,
        check_vma=False,
    )
```

time: 137 us -> 134 us (0.978)
  Pallas kernels: 19.3 us -> 12.6 us
  blocking collectives: 91.3 us -> 95.6 us
    pallas_call x3 -> x2, Pallas kernels: 14.3 us -> 7.6 us  [the longest x1 6.63 us: attend_own(): pl.pallas_call(own_kernel, in_specs=[SMEM_SPEC] + [VMEM_SPEC] * 2, out_sp...]
    all_to_all x3, blocking collectives: 91.3 us -> 95.6 us  [exchange(): lax.all_to_all(array, 'head', split_axis=0, concat_axis=0, tiled=True)]
  transfers between devices with their start and end apart: 3 -> 3, of which waited for: 1 -> 1; matrix products, arithmetic and copies ran while one was open for 1% -> 1% of each run, Pallas kernels for 9% -> 5%
where the time goes in v2:
time: 134 us; the launch traced here: 133 us
  blocking collectives  95.6 us (71%)
  waiting for transfers between devices  14 us (10%)
  Pallas kernels  12.6 us (9%)
  starting transfers between devices  7.54 us (6%)
  local copies, waits for them, and re-layouts  3.29 us (2%)
    all_to_all x3, blocking collectives, exchange(): lax.all_to_all(array, 'head', split_axis=0, concat_axis=0, tiled=True)  95.6 us
    all_to_all x1, waiting for transfers between devices, exchange(): lax.all_to_all(array, 'head', split_axis=0, concat_axis=0, tiled=True)  14 us
    pallas_call x1, Pallas kernels, attend_own(): pl.pallas_call(own_kernel, in_specs=[SMEM_SPEC] + [VMEM_SPEC] * 2, out_sp...  6.63 us
    all_to_all x1, starting transfers between devices, exchange(): lax.all_to_all(array, 'head', split_axis=0, concat_axis=0, tiled=True)  4.99 us
    pallas_call x1, Pallas kernels, prep(): pl.pallas_call(prep_kernel, grid=(steps,), in_specs=[wide, wide, wide, ga...  3.88 us
  transfers between devices with their start and end apart: 3, of which 1 were waited for; matrix products, arithmetic and copies ran while one was open for 1% of the time, Pallas kernels for 5%

profile of v2, /device:TPU:19, one launch (start us, length us, event | category | flops | bytes accessed | tf_op | source)
XLA Modules:
  0.0 133.5 jit_solution(7764992615895819369)
XLA Ops:
  0.0 3.9 %shard_map.64 = (bf16[32,128,128]{2,1,0:T(8,128)(2,1)}, bf16[32,2,128,128]{3,2,1,0:T(8,128)(2,1)}) custom-call(bf16[128,4096]{1,0:T(8,128)(2,1)} %queries_ref.1, bf16[128,4096]{1,0:T(8,128)(2,1)} %keys_ref.1, bf16[128,4096]{1,0:T(8,128)(2,1)} %values_ref.1, f32[1,128]{1,0:T(1,128)} %bitcast.17, f32[1,128]{1,0:T(1,128)} %bitcast.18), custom_call_target="tpu_custom_call" | custom-call | tf_op jit(solution)/shard_map/pallas_call | solution.py:53
  3.9 64.2 %conditional.1 = (bf16[32,2,128,128]{3,2,1,0:T(8,128)(2,1)S(1)}) conditional(s32[]{:T(128)} %convert_element_type.4, bf16[32,2,128,128]{3,2,1,0:T(8,128)(2,1)} %get-tuple-element.13, bf16[32,2,128,128]{3,2,1,0:T(8,128)(2,1)} %get-tuple-element.13), branch_computations={%region_0.1_spmd, %region_1.2_spmd} | conditional | flops 1048576 | bytes 16777224 | solution.py:225
  3.9 1.7 %slice_bitcast_fusion.1 = (bf16[32,128,128]{2,1,0:T(8,128)(2,1)S(1)}, bf16[32,128,128]{2,1,0:T(8,128)(2,1)S(1)}) fusion(bf16[32,2,128,128]{3,2,1,0:T(8,128)(2,1)} %param), kind=kLoop, calls=%fused_computation.2 | loop fusion | bytes 4194304 | tf_op jit(solution)/shard_map/cond/branch_0_fun/squeeze | solution.py:221
  5.6 39.1 %all_to_all.22 = bf16[32,128,128]{2,1,0:T(8,128)(2,1)S(1)} all-to-all(bf16[32,128,128]{2,1,0:T(8,128)(2,1)S(1)} %get-tuple-element.15), channel_id=1, replica_groups=mesh['slab'=8,'head'=32] {'head'}, dimensions={0} | all-to-all | bytes 2097152 | tf_op jit(solution)/shard_map/cond/branch_0_fun/all_to_all | solution.py:214
  44.7 23.1 %all_to_all.23 = bf16[32,128,128]{2,1,0:T(8,128)(2,1)S(1)} all-to-all(bf16[32,128,128]{2,1,0:T(8,128)(2,1)S(1)} %get-tuple-element.16), channel_id=1, replica_groups=mesh['slab'=8,'head'=32] {'head'}, dimensions={0} | all-to-all | bytes 2097152 | tf_op jit(solution)/shard_map/cond/branch_0_fun/all_to_all | solution.py:214
  67.7 0.2 pad_maximum_fusion
  67.9 0.1 copy.19
  68.1 0.0 copy-start.1
  68.1 5.0 %all-to-all-start.3 = ((bf16[32,128,128]{2,1,0:T(8,128)(2,1)}), bf16[32,128,128]{2,1,0:T(8,128)(2,1)S(1)}, u32[]{:S(2)}, u32[]{:S(2)}) async-start(bf16[32,128,128]{2,1,0:T(8,128)(2,1)} %get-tuple-element.12), calls=%async_computation.3 | async-start | bytes 2097152 | tf_op jit(solution)/shard_map/all_to_all | solution.py:214
  73.1 0.0 copy-start
  73.1 1.5 %constant_dynamic-slice_fusion = (bf16[16,2,128,128]{3,2,1,0:T(8,128)(2,1)}, bf16[16,2,128,128]{3,2,1,0:T(8,128)(2,1)}) fusion(bf16[32,2,128,128]{3,2,1,0:T(8,128)(2,1)S(1)} %get-tuple-element.14.kv_ref, s32[]{:T(128)S(6)} %select_n.15, s32[]{:T(128)S(6)} %select_n.14), kind=kLoop, calls=%fused_computation.4 | loop fusion | bytes 4194312 | tf_op jit(solution)/shard_map/dynamic_slice | solution.py:229
  74.6 0.0 copy-done.1
  74.6 1.9 %collective-permute-start.1 = (bf16[16,2,128,128]{3,2,1,0:T(8,128)(2,1)}, bf16[16,2,128,128]{3,2,1,0:T(8,128)(2,1)S(1)}, u32[]{:S(2)}, u32[]{:S(2)}) collective-permute-start(bf16[16,2,128,128]{3,2,1,0:T(8,128)(2,1)} %get-tuple-element.17), channel_id=1, source_target_pairs={{32,64},{96,128},{160,192},{64,32},{128,96},{192,160},{33,65},{97,... | collective-permute-start | bytes 3145736 | tf_op jit(solution)/shard_map/ppermute | solution.py:233
  76.5 0.6 collective-permute-start
  77.2 0.1 pad_add_fusion.place_ref
  77.2 14.0 %all-to-all-done.3.q_ref = bf16[32,128,128]{2,1,0:T(8,128)(2,1)S(1)} async-done(((bf16[32,128,128]{2,1,0:T(8,128)(2,1)}), bf16[32,128,128]{2,1,0:T(8,128)(2,1)S(1)}, u32[]{:S(2)}, u32[]{:S(2)}) %all-to-all-start.3) | async-done | bytes 1048608 | tf_op jit(solution)/shard_map/all_to_all | solution.py:214
  91.3 0.0 copy-done
  91.3 6.6 %shard_map.65.sums_ref = f32[32,128,256]{2,1,0:T(8,128)S(1)} custom-call(s32[1,3]{1,0:T(1,128)S(1)} %copy-done, bf16[32,128,128]{2,1,0:T(8,128)(2,1)S(1)} %all-to-all-done.3.q_ref, bf16[32,2,128,128]{3,2,1,0:T(8,128)(2,1)} %copy-done.1), custom_call_target="tpu_custom_call" | custom-call | flops 5033164800 | bytes 8388608 | tf_op jit(solution)/shard_map/pallas_call | solution.py:183
  97.9 0.0 collective-permute-done.1.far_ref
  97.9 0.0 collective-permute-done.near_ref
  97.9 1.0 shard_map.66
  98.9 33.5 %all_to_all.25.heads_ref = bf16[32,128,128]{2,1,0:T(8,128)(2,1)S(1)} all-to-all(bf16[32,128,128]{2,1,0:T(8,128)(2,1)S(1)} %shard_map.66), channel_id=1, replica_groups=mesh['slab'=8,'head'=32] {'head'}, dimensions={0} | all-to-all | bytes 2097152 | tf_op jit(solution)/shard_map/all_to_all | solution.py:214
  132.4 1.1 shard_map.67
Async XLA Ops:
  68.1 6.5 %copy-start.1 = (bf16[32,2,128,128]{3,2,1,0:T(8,128)(2,1)}, bf16[32,2,128,128]{3,2,1,0:T(8,128)(2,1)S(1)}, u32[]{:S(2)}) copy-start(bf16[32,2,128,128]{3,2,1,0:T(8,128)(2,1)S(1)} %get-tuple-element.14.kv_ref) | copy-start | bytes 6291460
  68.1 23.1 %all-to-all-start.3 = ((bf16[32,128,128]{2,1,0:T(8,128)(2,1)}), bf16[32,128,128]{2,1,0:T(8,128)(2,1)S(1)}, u32[]{:S(2)}, u32[]{:S(2)}) async-start(bf16[32,128,128]{2,1,0:T(8,128)(2,1)} %get-tuple-element.12), calls=%async_computation.3 | async-start | bytes 2097152 | tf_op jit(solution)/shard_map/all_to_all | solution.py:214
  73.1 18.1 %copy-start = (s32[1,3]{1,0:T(1,128)S(1)}, s32[1,3]{1,0:T(1,128)}, u32[]{:S(2)}) copy-start(s32[1,3]{1,0:T(1,128)} %windows_ref.3) | copy-start | bytes 40
  74.6 23.3 %collective-permute-start.1 = (bf16[16,2,128,128]{3,2,1,0:T(8,128)(2,1)}, bf16[16,2,128,128]{3,2,1,0:T(8,128)(2,1)S(1)}, u32[]{:S(2)}, u32[]{:S(2)}) collective-permute-start(bf16[16,2,128,128]{3,2,1,0:T(8,128)(2,1)} %get-tuple-element.17), channel_id=1, source_target_pairs={{32,64},{96,128},{160,192},{64,32},{128,96},{192,160},{33,65},{97,... | collective-permute-start | bytes 3145736 | tf_op jit(solution)/shard_map/ppermute | solution.py:233
  76.5 21.4 %collective-permute-start = (bf16[16,2,128,128]{3,2,1,0:T(8,128)(2,1)}, bf16[16,2,128,128]{3,2,1,0:T(8,128)(2,1)S(1)}, u32[]{:S(2)}, u32[]{:S(2)}) collective-permute-start(bf16[16,2,128,128]{3,2,1,0:T(8,128)(2,1)} %get-tuple-element.18), channel_id=1, source_target_pairs={{0,32},{64,96},{128,160},{192,224},{32,0},{96,64},{160,128},{224,1... | collective-permute-start | bytes 3145736 | tf_op jit(solution)/shard_map/ppermute | solution.py:233

commit v3 on v2

--- a/solution.py
+++ b/solution.py
@@ -16,6 +16,10 @@
 PREP_VMEM = 60 * 2**20
 SMALL_VMEM = 8 * 2**20
 ATTEND_VMEM = 16 * 2**20
+NEAR_COST = pl.CostEstimate(flops=0, bytes_accessed=0, transcendentals=0)
+FAR_COST = pl.CostEstimate(
+    flops=600 * TILE**3, bytes_accessed=2**22, transcendentals=100 * TILE**2
+)
 EXP2_SCALE = math.log2(math.e) / math.sqrt(TILE)
 F32 = jnp.float32
 BF16 = jnp.bfloat16
@@ -155,24 +159,22 @@
     for_each_window(windows_ref, run)
 
 
-def halo_kernel(place_ref, windows_ref, q_ref, near_ref, far_ref, sums_ref, out_ref):
-    halos = (
-        (near_ref, place_ref[0] * FRAME, 1.0),
-        (far_ref, place_ref[1] * FRAME, place_ref[2].astype(F32).astype(BF16)),
-    )
+def halo_kernel(place_ref, windows_ref, q_ref, halo_ref, sums_ref, base_ref, out_ref):
+    del base_ref
+    start = place_ref[0] * FRAME
+    ones = place_ref[1].astype(F32).astype(BF16)
 
     def run(wide_t, wide_r, wide_c):
         def visit(place, near_places):
-            for halo_ref, start, ones in halos:
-                both = sums_ref[start + place]
-                if wide_t:
-                    both = both + weighted_sums(
-                        q_ref[start + place],
-                        [halo_ref[n, KEY] for n in near_places],
-                        [halo_ref[n, VALUE] for n in near_places],
-                        ones,
-                    )
-                out_ref[start + place] = (both[:, :TILE] / both[:, TILE:]).astype(BF16)
+            both = sums_ref[start + place]
+            if wide_t:
+                both = both + weighted_sums(
+                    q_ref[start + place],
+                    [halo_ref[n, KEY] for n in near_places],
+                    [halo_ref[n, VALUE] for n in near_places],
+                    ones,
+                )
+            out_ref[start + place] = (both[:, :TILE] / both[:, TILE:]).astype(BF16)
 
         for_each_place(wide_r, wide_c, wide_t and wide_r and wide_c, visit)
 
@@ -192,17 +194,16 @@
     )(windows, q, kv)
 
 
-def attend_halos(place, windows, q, near, far, sums):
+def attend_halo(place, windows, q, halo, sums, base, cost):
     return pl.pallas_call(
         halo_kernel,
         in_specs=[SMEM_SPEC, SMEM_SPEC] + [VMEM_SPEC] * 4,
         out_specs=VMEM_SPEC,
         out_shape=jax.ShapeDtypeStruct(q.shape, BF16),
+        input_output_aliases={5: 0},
         compiler_params=pltpu.CompilerParams(vmem_limit_bytes=ATTEND_VMEM),
-        cost_estimate=pl.CostEstimate(
-            flops=200 * 6 * TILE**3, bytes_accessed=2**23, transcendentals=200 * TILE**2
-        ),
-    )(place, windows, q, near, far, sums)
+        cost_estimate=cost,
+    )(place, windows, q, halo, sums, base)
 
 
 def on_device(queries, keys, values, q_gain, k_gain, windows):
@@ -236,8 +237,10 @@
     near = swap(frame_of(1 - odd), 0, slabs)
     far_present = ((slab > 0) & (slab < slabs - 1)).astype(jnp.int32)
     sums = attend_own(windows, q, kv)
-    place = jnp.stack([1 - odd, odd, far_present])
-    return merge_heads(exchange(attend_halos(place, windows, q, near, far, sums)))
+    result = jnp.zeros(q.shape, BF16)
+    result = attend_halo(jnp.stack([1 - odd, 1]), windows, q, near, sums, result, NEAR_COST)
+    result = attend_halo(jnp.stack([odd, far_present]), windows, q, far, sums, result, FAR_COST)
+    return merge_heads(exchange(result))
 
 
 def solution(mesh):

time: 134 us -> 135 us (level)
  Pallas kernels: 12.6 us -> 16.6 us
  blocking collectives: 95.6 us -> 92.6 us
    pallas_call x1 -> x2, Pallas kernels: 0.97 us -> 7.55 us  [attend_halo(): pl.pallas_call(halo_kernel, in_specs=[SMEM_SPEC, SMEM_SPEC] + [VMEM_SPEC]...]
    all_to_all x3, blocking collectives: 95.6 us -> 92.6 us  [exchange(): lax.all_to_all(array, 'head', split_axis=0, concat_axis=0, tiled=True)]
    pallas_call x1, Pallas kernels: 6.63 us -> 4.05 us  [attend_own(): pl.pallas_call(own_kernel, in_specs=[SMEM_SPEC] + [VMEM_SPEC] * 2, out_sp...]
  transfers between devices with their start and end apart: 3 -> 3, of which waited for: 1 -> 1; matrix products, arithmetic and copies ran while one was open for 1% -> 1% of each run, Pallas kernels for 5% -> 6%
where the time goes in v3:
time: 135 us
  blocking collectives  92.6 us (69%)
  Pallas kernels  16.6 us (12%)
  waiting for transfers between devices  13.2 us (10%)
  starting transfers between devices  8.29 us (6%)
  local copies, waits for them, and re-layouts  3.52 us (3%)
    all_to_all x3, blocking collectives, exchange(): lax.all_to_all(array, 'head', split_axis=0, concat_axis=0, tiled=True)  92.6 us
    all_to_all x1, waiting for transfers between devices, exchange(): lax.all_to_all(array, 'head', split_axis=0, concat_axis=0, tiled=True)  13.2 us
    pallas_call x2, Pallas kernels, attend_halo(): pl.pallas_call(halo_kernel, in_specs=[SMEM_SPEC, SMEM_SPEC] + [VMEM_SPEC]...  7.55 us
    all_to_all x1, starting transfers between devices, exchange(): lax.all_to_all(array, 'head', split_axis=0, concat_axis=0, tiled=True)  4.99 us
    pallas_call x1, Pallas kernels, attend_own(): pl.pallas_call(own_kernel, in_specs=[SMEM_SPEC] + [VMEM_SPEC] * 2, out_sp...  4.05 us
    pallas_call x1, Pallas kernels, prep(): pl.pallas_call(prep_kernel, grid=(steps,), in_specs=[wide, wide, wide, ga...  3.88 us
    ppermute x2, starting transfers between devices, swap(): return lax.ppermute(block, 'slab', pairs + [(b, a) for a, b in pairs])  3.29 us
  transfers between devices with their start and end apart: 3, of which 1 were waited for; matrix products, arithmetic and copies ran while one was open for 1% of the time, Pallas kernels for 6%

profile of v3, /device:TPU:19, one launch (start us, length us, event | category | flops | bytes accessed | tf_op | source)
XLA Modules:
  0.0 134.7 jit_solution(14925735718730532419)
XLA Ops:
  0.0 3.9 %shard_map.64 = (bf16[32,128,128]{2,1,0:T(8,128)(2,1)}, bf16[32,2,128,128]{3,2,1,0:T(8,128)(2,1)}) custom-call(bf16[128,4096]{1,0:T(8,128)(2,1)} %queries_ref.1, bf16[128,4096]{1,0:T(8,128)(2,1)} %keys_ref.1, bf16[128,4096]{1,0:T(8,128)(2,1)} %values_ref.1, f32[1,128]{1,0:T(1,128)} %bitcast.17, f32[1,128]{1,0:T(1,128)} %bitcast.18), custom_call_target="tpu_custom_call" | custom-call | tf_op jit(solution)/shard_map/pallas_call | solution.py:57
  3.9 64.2 %conditional.1 = (bf16[32,2,128,128]{3,2,1,0:T(8,128)(2,1)S(1)}) conditional(s32[]{:T(128)} %convert_element_type.4, bf16[32,2,128,128]{3,2,1,0:T(8,128)(2,1)} %get-tuple-element.13, bf16[32,2,128,128]{3,2,1,0:T(8,128)(2,1)} %get-tuple-element.13), branch_computations={%region_0.1_spmd, %region_1.2_spmd} | conditional | flops 1048576 | bytes 16777224 | solution.py:226
  3.9 1.7 %slice_bitcast_fusion.1 = (bf16[32,128,128]{2,1,0:T(8,128)(2,1)S(1)}, bf16[32,128,128]{2,1,0:T(8,128)(2,1)S(1)}) fusion(bf16[32,2,128,128]{3,2,1,0:T(8,128)(2,1)} %param), kind=kLoop, calls=%fused_computation.2 | loop fusion | bytes 4194304 | tf_op jit(solution)/shard_map/cond/branch_0_fun/squeeze | solution.py:222
  5.6 39.1 %all_to_all.22 = bf16[32,128,128]{2,1,0:T(8,128)(2,1)S(1)} all-to-all(bf16[32,128,128]{2,1,0:T(8,128)(2,1)S(1)} %get-tuple-element.16), channel_id=1, replica_groups=mesh['slab'=8,'head'=32] {'head'}, dimensions={0} | all-to-all | bytes 2097152 | tf_op jit(solution)/shard_map/cond/branch_0_fun/all_to_all | solution.py:215
  44.7 23.1 %all_to_all.23 = bf16[32,128,128]{2,1,0:T(8,128)(2,1)S(1)} all-to-all(bf16[32,128,128]{2,1,0:T(8,128)(2,1)S(1)} %get-tuple-element.15), channel_id=1, replica_groups=mesh['slab'=8,'head'=32] {'head'}, dimensions={0} | all-to-all | bytes 2097152 | tf_op jit(solution)/shard_map/cond/branch_0_fun/all_to_all | solution.py:215
  67.7 0.2 pad_maximum_fusion
  67.9 0.1 copy.21
  68.1 0.0 copy-start.1
  68.1 5.0 %all-to-all-start.3 = ((bf16[32,128,128]{2,1,0:T(8,128)(2,1)}), bf16[32,128,128]{2,1,0:T(8,128)(2,1)S(1)}, u32[]{:S(2)}, u32[]{:S(2)}) async-start(bf16[32,128,128]{2,1,0:T(8,128)(2,1)} %get-tuple-element.12), calls=%async_computation.3 | async-start | bytes 2097152 | tf_op jit(solution)/shard_map/all_to_all | solution.py:215
  73.1 0.0 copy-start
  73.1 1.5 %constant_dynamic-slice_fusion = (bf16[16,2,128,128]{3,2,1,0:T(8,128)(2,1)}, bf16[16,2,128,128]{3,2,1,0:T(8,128)(2,1)}) fusion(bf16[32,2,128,128]{3,2,1,0:T(8,128)(2,1)S(1)} %get-tuple-element.14.kv_ref, s32[]{:T(128)S(6)} %select_n.15, s32[]{:T(128)S(6)} %select_n.14), kind=kLoop, calls=%fused_computation.5 | loop fusion | bytes 4194312 | tf_op jit(solution)/shard_map/dynamic_slice | solution.py:230
  74.6 0.0 copy-done.1
  74.6 0.0 collective-permute-start.1
  74.6 3.3 %collective-permute-start = (bf16[16,2,128,128]{3,2,1,0:T(8,128)(2,1)}, bf16[16,2,128,128]{3,2,1,0:T(8,128)(2,1)S(1)}, u32[]{:S(2)}, u32[]{:S(2)}) collective-permute-start(bf16[16,2,128,128]{3,2,1,0:T(8,128)(2,1)} %get-tuple-element.18), channel_id=1, source_target_pairs={{32,64},{96,128},{160,192},{64,32},{128,96},{192,160},{33,65},{97,... | collective-permute-start | bytes 3145736 | tf_op jit(solution)/shard_map/ppermute | solution.py:234
  77.9 0.1 pad_add_fusion.place_ref
  78.0 0.1 pad_add_fusion.1.place_ref
  78.1 13.2 %all-to-all-done.3.q_ref = bf16[32,128,128]{2,1,0:T(8,128)(2,1)S(1)} async-done(((bf16[32,128,128]{2,1,0:T(8,128)(2,1)}), bf16[32,128,128]{2,1,0:T(8,128)(2,1)S(1)}, u32[]{:S(2)}, u32[]{:S(2)}) %all-to-all-start.3) | async-done | bytes 1048608 | tf_op jit(solution)/shard_map/all_to_all | solution.py:215
  91.3 0.0 copy-done
  91.3 4.0 %shard_map.65.sums_ref = f32[32,128,256]{2,1,0:T(8,128)S(1)} custom-call(s32[1,3]{1,0:T(1,128)S(1)} %copy-done, bf16[32,128,128]{2,1,0:T(8,128)(2,1)S(1)} %all-to-all-done.3.q_ref, bf16[32,2,128,128]{3,2,1,0:T(8,128)(2,1)} %copy-done.1), custom_call_target="tpu_custom_call" | custom-call | flops 5033164800 | bytes 8388608 | tf_op jit(solution)/shard_map/pallas_call | solution.py:185
  95.3 0.0 collective-permute-done.1.halo_ref
  95.3 0.2 broadcast_in_dim.3.base_ref
  95.6 3.8 %shard_map.66.base_ref = bf16[32,128,128]{2,1,0:T(8,128)(2,1)S(1)} custom-call(s32[2]{0:T(128)S(1)} %pad_add_fusion.1.place_ref, s32[1,3]{1,0:T(1,128)S(1)} %copy-done, bf16[32,128,128]{2,1,0:T(8,128)(2,1)S(1)} %all-to-all-done.3.q_ref, bf16[16,2,128,128]{3,2,1,0:T(8,128)(2,1)S(1)} %collective-permute-done.1.halo_ref, ...), custom_call_target="tpu_custom_call", output_to_operand_aliasing={{}: (5, {})} | custom-call | tf_op jit(solution)/shard_map/pallas_call | solution.py:198
  99.3 0.0 collective-permute-done.halo_ref
  99.4 3.8 %shard_map.67 = bf16[32,128,128]{2,1,0:T(8,128)(2,1)S(1)} custom-call(s32[2]{0:T(128)S(1)} %pad_add_fusion.place_ref, s32[1,3]{1,0:T(1,128)S(1)} %copy-done, bf16[32,128,128]{2,1,0:T(8,128)(2,1)S(1)} %all-to-all-done.3.q_ref, bf16[16,2,128,128]{3,2,1,0:T(8,128)(2,1)S(1)} %collective-permute-done.halo_ref, ...), custom_call_target="tpu_custom_call", output_to_operand_aliasing={{}: (5, {})} | custom-call | flops 1258291200 | bytes 4194304 | tf_op jit(solution)/shard_map/pallas_call | solution.py:198
  103.1 30.4 %all_to_all.25.heads_ref = bf16[32,128,128]{2,1,0:T(8,128)(2,1)S(1)} all-to-all(bf16[32,128,128]{2,1,0:T(8,128)(2,1)S(1)} %shard_map.67), channel_id=1, replica_groups=mesh['slab'=8,'head'=32] {'head'}, dimensions={0} | all-to-all | bytes 2097152 | tf_op jit(solution)/shard_map/all_to_all | solution.py:215
  133.6 1.1 shard_map.68
Async XLA Ops:
  68.1 6.5 %copy-start.1 = (bf16[32,2,128,128]{3,2,1,0:T(8,128)(2,1)}, bf16[32,2,128,128]{3,2,1,0:T(8,128)(2,1)S(1)}, u32[]{:S(2)}) copy-start(bf16[32,2,128,128]{3,2,1,0:T(8,128)(2,1)S(1)} %get-tuple-element.14.kv_ref) | copy-start | bytes 6291460
  68.1 23.1 %all-to-all-start.3 = ((bf16[32,128,128]{2,1,0:T(8,128)(2,1)}), bf16[32,128,128]{2,1,0:T(8,128)(2,1)S(1)}, u32[]{:S(2)}, u32[]{:S(2)}) async-start(bf16[32,128,128]{2,1,0:T(8,128)(2,1)} %get-tuple-element.12), calls=%async_computation.3 | async-start | bytes 2097152 | tf_op jit(solution)/shard_map/all_to_all | solution.py:215
  73.1 18.1 %copy-start = (s32[1,3]{1,0:T(1,128)S(1)}, s32[1,3]{1,0:T(1,128)}, u32[]{:S(2)}) copy-start(s32[1,3]{1,0:T(1,128)} %windows_ref.5) | copy-start | bytes 40
  74.6 20.7 %collective-permute-start.1 = (bf16[16,2,128,128]{3,2,1,0:T(8,128)(2,1)}, bf16[16,2,128,128]{3,2,1,0:T(8,128)(2,1)S(1)}, u32[]{:S(2)}, u32[]{:S(2)}) collective-permute-start(bf16[16,2,128,128]{3,2,1,0:T(8,128)(2,1)} %get-tuple-element.17), channel_id=1, source_target_pairs={{0,32},{64,96},{128,160},{192,224},{32,0},{96,64},{160,128},{224,1... | collective-permute-start | bytes 3145736 | tf_op jit(solution)/shard_map/ppermute | solution.py:234
  74.6 24.7 %collective-permute-start = (bf16[16,2,128,128]{3,2,1,0:T(8,128)(2,1)}, bf16[16,2,128,128]{3,2,1,0:T(8,128)(2,1)S(1)}, u32[]{:S(2)}, u32[]{:S(2)}) collective-permute-start(bf16[16,2,128,128]{3,2,1,0:T(8,128)(2,1)} %get-tuple-element.18), channel_id=1, source_target_pairs={{32,64},{96,128},{160,192},{64,32},{128,96},{192,160},{33,65},{97,... | collective-permute-start | bytes 3145736 | tf_op jit(solution)/shard_map/ppermute | solution.py:234

commit v4 on v3

--- a/solution.py
+++ b/solution.py
@@ -159,8 +159,11 @@
     for_each_window(windows_ref, run)
 
 
-def halo_kernel(place_ref, windows_ref, q_ref, halo_ref, sums_ref, base_ref, out_ref):
-    del base_ref
+def halo_kernel(place_ref, windows_ref, q_ref, halo_ref, sums_ref, *results):
+    out_ref = results[-1]
+    for base_ref in results[:-1]:
+        other = FRAME - place_ref[0] * FRAME
+        out_ref[pl.ds(other, FRAME)] = base_ref[pl.ds(other, FRAME)]
     start = place_ref[0] * FRAME
     ones = place_ref[1].astype(F32).astype(BF16)
 
@@ -194,16 +197,15 @@
     )(windows, q, kv)
 
 
-def attend_halo(place, windows, q, halo, sums, base, cost):
+def attend_halo(place, windows, q, halo, sums, cost, base=()):
     return pl.pallas_call(
         halo_kernel,
-        in_specs=[SMEM_SPEC, SMEM_SPEC] + [VMEM_SPEC] * 4,
+        in_specs=[SMEM_SPEC, SMEM_SPEC] + [VMEM_SPEC] * (3 + len(base)),
         out_specs=VMEM_SPEC,
         out_shape=jax.ShapeDtypeStruct(q.shape, BF16),
-        input_output_aliases={5: 0},
         compiler_params=pltpu.CompilerParams(vmem_limit_bytes=ATTEND_VMEM),
         cost_estimate=cost,
-    )(place, windows, q, halo, sums, base)
+    )(place, windows, q, halo, sums, *base)
 
 
 def on_device(queries, keys, values, q_gain, k_gain, windows):
@@ -237,9 +239,8 @@
     near = swap(frame_of(1 - odd), 0, slabs)
     far_present = ((slab > 0) & (slab < slabs - 1)).astype(jnp.int32)
     sums = attend_own(windows, q, kv)
-    result = jnp.zeros(q.shape, BF16)
-    result = attend_halo(jnp.stack([1 - odd, 1]), windows, q, near, sums, result, NEAR_COST)
-    result = attend_halo(jnp.stack([odd, far_present]), windows, q, far, sums, result, FAR_COST)
+    result = attend_halo(jnp.stack([1 - odd, 1]), windows, q, near, sums, NEAR_COST)
+    result = attend_halo(jnp.stack([odd, far_present]), windows, q, far, sums, FAR_COST, (result,))
     return merge_heads(exchange(result))
 
 

time: 135 us -> 134 us (level)
  Pallas kernels: 16.6 us -> 12.4 us
  blocking collectives: 92.6 us -> 96.7 us
    pallas_call x2, Pallas kernels: 7.55 us -> 1.7 us  [attend_halo(): pl.pallas_call(halo_kernel, in_specs=[SMEM_SPEC, SMEM_SPEC] + [VMEM_SPEC]...]
    all_to_all x3, blocking collectives: 92.6 us -> 96.7 us  [exchange(): lax.all_to_all(array, 'head', split_axis=0, concat_axis=0, tiled=True)]
    pallas_call x1, Pallas kernels: 4.05 us -> 5.7 us  [attend_own(): pl.pallas_call(own_kernel, in_specs=[SMEM_SPEC] + [VMEM_SPEC] * 2, out_sp...]
  transfers between devices with their start and end apart: 3 -> 3, of which waited for: 1 -> 1; matrix products, arithmetic and copies ran while one was open for 1% -> 1% of each run, Pallas kernels for 6% -> 5%
where the time goes in v4:
time: 134 us
  blocking collectives  96.7 us (72%)
  waiting for transfers between devices  13.2 us (10%)
  Pallas kernels  12.4 us (9%)
  starting transfers between devices  8.29 us (6%)
  local copies, waits for them, and re-layouts  3.29 us (2%)
    all_to_all x3, blocking collectives, exchange(): lax.all_to_all(array, 'head', split_axis=0, concat_axis=0, tiled=True)  96.7 us
    all_to_all x1, waiting for transfers between devices, exchange(): lax.all_to_all(array, 'head', split_axis=0, concat_axis=0, tiled=True)  13.2 us
    pallas_call x1, Pallas kernels, attend_own(): pl.pallas_call(own_kernel, in_specs=[SMEM_SPEC] + [VMEM_SPEC] * 2, out_sp...  5.7 us
    all_to_all x1, starting transfers between devices, exchange(): lax.all_to_all(array, 'head', split_axis=0, concat_axis=0, tiled=True)  4.99 us
    pallas_call x1, Pallas kernels, prep(): pl.pallas_call(prep_kernel, grid=(steps,), in_specs=[wide, wide, wide, ga...  3.88 us
    ppermute x2, starting transfers between devices, swap(): return lax.ppermute(block, 'slab', pairs + [(b, a) for a, b in pairs])  3.29 us
  transfers between devices with their start and end apart: 3, of which 1 were waited for; matrix products, arithmetic and copies ran while one was open for 1% of the time, Pallas kernels for 5%

profile of v4, /device:TPU:19, one launch (start us, length us, event | category | flops | bytes accessed | tf_op | source)
XLA Modules:
  0.0 134.3 jit_solution(11494035276665253020)
XLA Ops:
  0.0 3.9 %shard_map.64 = (bf16[32,128,128]{2,1,0:T(8,128)(2,1)}, bf16[32,2,128,128]{3,2,1,0:T(8,128)(2,1)}) custom-call(bf16[128,4096]{1,0:T(8,128)(2,1)} %queries_ref.1, bf16[128,4096]{1,0:T(8,128)(2,1)} %keys_ref.1, bf16[128,4096]{1,0:T(8,128)(2,1)} %values_ref.1, f32[1,128]{1,0:T(1,128)} %bitcast.17, f32[1,128]{1,0:T(1,128)} %bitcast.18), custom_call_target="tpu_custom_call" | custom-call | tf_op jit(solution)/shard_map/pallas_call | solution.py:57
  3.9 64.2 %conditional.1 = (bf16[32,2,128,128]{3,2,1,0:T(8,128)(2,1)S(1)}) conditional(s32[]{:T(128)} %convert_element_type.4, bf16[32,2,128,128]{3,2,1,0:T(8,128)(2,1)} %get-tuple-element.13, bf16[32,2,128,128]{3,2,1,0:T(8,128)(2,1)} %get-tuple-element.13), branch_computations={%region_0.1_spmd, %region_1.2_spmd} | conditional | flops 1048576 | bytes 16777224 | solution.py:228
  3.9 1.7 %slice_bitcast_fusion.1 = (bf16[32,128,128]{2,1,0:T(8,128)(2,1)S(1)}, bf16[32,128,128]{2,1,0:T(8,128)(2,1)S(1)}) fusion(bf16[32,2,128,128]{3,2,1,0:T(8,128)(2,1)} %param), kind=kLoop, calls=%fused_computation.2 | loop fusion | bytes 4194304 | tf_op jit(solution)/shard_map/cond/branch_0_fun/squeeze | solution.py:224
  5.6 39.1 %all_to_all.22 = bf16[32,128,128]{2,1,0:T(8,128)(2,1)S(1)} all-to-all(bf16[32,128,128]{2,1,0:T(8,128)(2,1)S(1)} %get-tuple-element.15), channel_id=1, replica_groups=mesh['slab'=8,'head'=32] {'head'}, dimensions={0} | all-to-all | bytes 2097152 | tf_op jit(solution)/shard_map/cond/branch_0_fun/all_to_all | solution.py:217
  44.7 23.1 %all_to_all.23 = bf16[32,128,128]{2,1,0:T(8,128)(2,1)S(1)} all-to-all(bf16[32,128,128]{2,1,0:T(8,128)(2,1)S(1)} %get-tuple-element.16), channel_id=1, replica_groups=mesh['slab'=8,'head'=32] {'head'}, dimensions={0} | all-to-all | bytes 2097152 | tf_op jit(solution)/shard_map/cond/branch_0_fun/all_to_all | solution.py:217
  67.7 0.2 pad_maximum_fusion
  67.9 0.1 copy.19
  68.1 0.0 copy-start.1
  68.1 5.0 %all-to-all-start.3 = ((bf16[32,128,128]{2,1,0:T(8,128)(2,1)}), bf16[32,128,128]{2,1,0:T(8,128)(2,1)S(1)}, u32[]{:S(2)}, u32[]{:S(2)}) async-start(bf16[32,128,128]{2,1,0:T(8,128)(2,1)} %get-tuple-element.12), calls=%async_computation.3 | async-start | bytes 2097152 | tf_op jit(solution)/shard_map/all_to_all | solution.py:217
  73.1 0.0 copy-start
  73.1 1.5 %constant_dynamic-slice_fusion = (bf16[16,2,128,128]{3,2,1,0:T(8,128)(2,1)}, bf16[16,2,128,128]{3,2,1,0:T(8,128)(2,1)}) fusion(bf16[32,2,128,128]{3,2,1,0:T(8,128)(2,1)S(1)} %get-tuple-element.14.kv_ref, s32[]{:T(128)S(6)} %select_n.15, s32[]{:T(128)S(6)} %select_n.14), kind=kLoop, calls=%fused_computation.5 | loop fusion | bytes 4194312 | tf_op jit(solution)/shard_map/dynamic_slice | solution.py:232
  74.6 0.0 copy-done.1
  74.6 0.0 collective-permute-start.1
  74.6 3.3 %collective-permute-start = (bf16[16,2,128,128]{3,2,1,0:T(8,128)(2,1)}, bf16[16,2,128,128]{3,2,1,0:T(8,128)(2,1)S(1)}, u32[]{:S(2)}, u32[]{:S(2)}) collective-permute-start(bf16[16,2,128,128]{3,2,1,0:T(8,128)(2,1)} %get-tuple-element.18), channel_id=1, source_target_pairs={{32,64},{96,128},{160,192},{64,32},{128,96},{192,160},{33,65},{97,... | collective-permute-start | bytes 3145736 | tf_op jit(solution)/shard_map/ppermute | solution.py:236
  77.9 0.1 pad_add_fusion.place_ref
  78.0 0.1 pad_add_fusion.1.place_ref
  78.1 13.2 %all-to-all-done.3.q_ref = bf16[32,128,128]{2,1,0:T(8,128)(2,1)S(1)} async-done(((bf16[32,128,128]{2,1,0:T(8,128)(2,1)}), bf16[32,128,128]{2,1,0:T(8,128)(2,1)S(1)}, u32[]{:S(2)}, u32[]{:S(2)}) %all-to-all-start.3) | async-done | bytes 1048608 | tf_op jit(solution)/shard_map/all_to_all | solution.py:217
  91.3 0.0 copy-done
  91.3 5.7 %shard_map.65.sums_ref = f32[32,128,256]{2,1,0:T(8,128)S(1)} custom-call(s32[1,3]{1,0:T(1,128)S(1)} %copy-done, bf16[32,128,128]{2,1,0:T(8,128)(2,1)S(1)} %all-to-all-done.3.q_ref, bf16[32,2,128,128]{3,2,1,0:T(8,128)(2,1)} %copy-done.1), custom_call_target="tpu_custom_call" | custom-call | flops 5033164800 | bytes 8388608 | tf_op jit(solution)/shard_map/pallas_call | solution.py:188
  97.0 0.0 collective-permute-done.1.halo_ref
  97.0 0.8 shard_map.66.results_0_
  97.8 0.0 collective-permute-done.halo_ref
  97.8 0.9 shard_map.67
  98.7 34.5 %all_to_all.25.heads_ref = bf16[32,128,128]{2,1,0:T(8,128)(2,1)S(1)} all-to-all(bf16[32,128,128]{2,1,0:T(8,128)(2,1)S(1)} %shard_map.67), channel_id=1, replica_groups=mesh['slab'=8,'head'=32] {'head'}, dimensions={0} | all-to-all | bytes 2097152 | tf_op jit(solution)/shard_map/all_to_all | solution.py:217
  133.2 1.1 shard_map.68
Async XLA Ops:
  68.1 6.5 %copy-start.1 = (bf16[32,2,128,128]{3,2,1,0:T(8,128)(2,1)}, bf16[32,2,128,128]{3,2,1,0:T(8,128)(2,1)S(1)}, u32[]{:S(2)}) copy-start(bf16[32,2,128,128]{3,2,1,0:T(8,128)(2,1)S(1)} %get-tuple-element.14.kv_ref) | copy-start | bytes 6291460
  68.1 23.1 %all-to-all-start.3 = ((bf16[32,128,128]{2,1,0:T(8,128)(2,1)}), bf16[32,128,128]{2,1,0:T(8,128)(2,1)S(1)}, u32[]{:S(2)}, u32[]{:S(2)}) async-start(bf16[32,128,128]{2,1,0:T(8,128)(2,1)} %get-tuple-element.12), calls=%async_computation.3 | async-start | bytes 2097152 | tf_op jit(solution)/shard_map/all_to_all | solution.py:217
  73.1 18.1 %copy-start = (s32[1,3]{1,0:T(1,128)S(1)}, s32[1,3]{1,0:T(1,128)}, u32[]{:S(2)}) copy-start(s32[1,3]{1,0:T(1,128)} %windows_ref.5) | copy-start | bytes 40
  74.6 22.4 %collective-permute-start.1 = (bf16[16,2,128,128]{3,2,1,0:T(8,128)(2,1)}, bf16[16,2,128,128]{3,2,1,0:T(8,128)(2,1)S(1)}, u32[]{:S(2)}, u32[]{:S(2)}) collective-permute-start(bf16[16,2,128,128]{3,2,1,0:T(8,128)(2,1)} %get-tuple-element.17), channel_id=1, source_target_pairs={{0,32},{64,96},{128,160},{192,224},{32,0},{96,64},{160,128},{224,1... | collective-permute-start | bytes 3145736 | tf_op jit(solution)/shard_map/ppermute | solution.py:236
  74.6 23.2 %collective-permute-start = (bf16[16,2,128,128]{3,2,1,0:T(8,128)(2,1)}, bf16[16,2,128,128]{3,2,1,0:T(8,128)(2,1)S(1)}, u32[]{:S(2)}, u32[]{:S(2)}) collective-permute-start(bf16[16,2,128,128]{3,2,1,0:T(8,128)(2,1)} %get-tuple-element.18), channel_id=1, source_target_pairs={{32,64},{96,128},{160,192},{64,32},{128,96},{192,160},{33,65},{97,... | collective-permute-start | bytes 3145736 | tf_op jit(solution)/shard_map/ppermute | solution.py:236

commit v5 on v4

--- a/solution.py
+++ b/solution.py
@@ -220,8 +220,9 @@
         return exchange(kv)
 
     def apart(kv):
-        v = exchange(kv[:, VALUE])
-        k = exchange(kv[:, KEY])
+        v, rest = lax.optimization_barrier((kv[:, VALUE], kv))
+        v = exchange(v)
+        k = exchange(rest[:, KEY])
         return jnp.stack([k, v], axis=1)
 
     q, kv = prep(queries, keys, values, q_gain, k_gain)

time: 134 us -> 135 us (level)
  blocking collectives: 96.7 us -> 89.6 us
  Pallas kernels: 12.4 us -> 19.5 us
    all_to_all x3, blocking collectives: 96.7 us -> 89.6 us  [exchange(): lax.all_to_all(array, 'head', split_axis=0, concat_axis=0, tiled=True)]
    pallas_call x2, Pallas kernels: 1.7 us -> 5.49 us  [attend_halo(): pl.pallas_call(halo_kernel, in_specs=[SMEM_SPEC, SMEM_SPEC] + [VMEM_SPEC]...]
    pallas_call x1, Pallas kernels: 5.7 us -> 9.04 us  [attend_own(): pl.pallas_call(own_kernel, in_specs=[SMEM_SPEC] + [VMEM_SPEC] * 2, out_sp...]
  transfers between devices with their start and end apart: 3 -> 3, of which waited for: 1 -> 1; matrix products, arithmetic and copies ran while one was open for 1% -> 1% of each run, Pallas kernels for 5% -> 9%
where the time goes in v5:
time: 135 us
  blocking collectives  89.6 us (66%)
  Pallas kernels  19.5 us (14%)
  waiting for transfers between devices  12.4 us (9%)
  starting transfers between devices  8.34 us (6%)
  local copies, waits for them, and re-layouts  4.19 us (3%)
    all_to_all x3, blocking collectives, exchange(): lax.all_to_all(array, 'head', split_axis=0, concat_axis=0, tiled=True)  89.6 us
    all_to_all x1, waiting for transfers between devices, exchange(): lax.all_to_all(array, 'head', split_axis=0, concat_axis=0, tiled=True)  12.4 us
    pallas_call x1, Pallas kernels, attend_own(): pl.pallas_call(own_kernel, in_specs=[SMEM_SPEC] + [VMEM_SPEC] * 2, out_sp...  9.04 us
    pallas_call x2, Pallas kernels, attend_halo(): pl.pallas_call(halo_kernel, in_specs=[SMEM_SPEC, SMEM_SPEC] + [VMEM_SPEC]...  5.49 us
    all_to_all x1, starting transfers between devices, exchange(): lax.all_to_all(array, 'head', split_axis=0, concat_axis=0, tiled=True)  5.05 us
    pallas_call x1, Pallas kernels, prep(): pl.pallas_call(prep_kernel, grid=(steps,), in_specs=[wide, wide, wide, ga...  3.88 us
    ppermute x2, starting transfers between devices, swap(): return lax.ppermute(block, 'slab', pairs + [(b, a) for a, b in pairs])  3.29 us
  transfers between devices with their start and end apart: 3, of which 1 were waited for; matrix products, arithmetic and copies ran while one was open for 1% of the time, Pallas kernels for 9%

profile of v5, /device:TPU:19, one launch (start us, length us, event | category | flops | bytes accessed | tf_op | source)
XLA Modules:
  0.0 134.6 jit_solution(494790327767009414)
XLA Ops:
  0.0 3.9 %shard_map.64 = (bf16[32,128,128]{2,1,0:T(8,128)(2,1)}, bf16[32,2,128,128]{3,2,1,0:T(8,128)(2,1)}) custom-call(bf16[128,4096]{1,0:T(8,128)(2,1)} %queries_ref.1, bf16[128,4096]{1,0:T(8,128)(2,1)} %keys_ref.1, bf16[128,4096]{1,0:T(8,128)(2,1)} %values_ref.1, f32[1,128]{1,0:T(1,128)} %bitcast.15, f32[1,128]{1,0:T(1,128)} %bitcast.16), custom_call_target="tpu_custom_call" | custom-call | tf_op jit(solution)/shard_map/pallas_call | solution.py:57
  3.9 65.7 %conditional.1 = (bf16[32,2,128,128]{3,2,1,0:T(8,128)(2,1)S(1)}) conditional(s32[]{:T(128)} %convert_element_type.4, bf16[32,2,128,128]{3,2,1,0:T(8,128)(2,1)} %get-tuple-element.15, bf16[32,2,128,128]{3,2,1,0:T(8,128)(2,1)} %get-tuple-element.15), branch_computations={%region_0.1_spmd, %region_1.2_spmd} | conditional | flops 1048576 | bytes 16777224 | solution.py:229
  3.9 1.3 slice_bitcast_fusion.1
  5.2 1.3 slice_bitcast_fusion
  6.5 39.3 %all_to_all.22 = bf16[32,128,128]{2,1,0:T(8,128)(2,1)S(1)} all-to-all(bf16[32,128,128]{2,1,0:T(8,128)(2,1)S(1)} %slice_bitcast_fusion), channel_id=1, replica_groups=mesh['slab'=8,'head'=32] {'head'}, dimensions={0} | all-to-all | bytes 2097152 | tf_op jit(solution)/shard_map/cond/branch_0_fun/all_to_all | solution.py:217
  45.8 23.4 %all_to_all.23 = bf16[32,128,128]{2,1,0:T(8,128)(2,1)S(1)} all-to-all(bf16[32,128,128]{2,1,0:T(8,128)(2,1)S(1)} %slice_bitcast_fusion.1), channel_id=1, replica_groups=mesh['slab'=8,'head'=32] {'head'}, dimensions={0} | all-to-all | bytes 2097152 | tf_op jit(solution)/shard_map/cond/branch_0_fun/all_to_all | solution.py:217
  69.2 0.2 pad_maximum_fusion
  69.4 0.1 copy.19
  69.5 0.0 copy-start.1
  69.6 5.0 %all-to-all-start.3 = ((bf16[32,128,128]{2,1,0:T(8,128)(2,1)}), bf16[32,128,128]{2,1,0:T(8,128)(2,1)S(1)}, u32[]{:S(2)}, u32[]{:S(2)}) async-start(bf16[32,128,128]{2,1,0:T(8,128)(2,1)} %get-tuple-element.14), calls=%async_computation.3 | async-start | bytes 2097152 | tf_op jit(solution)/shard_map/all_to_all | solution.py:217
  74.6 0.0 copy-start
  74.6 1.4 %constant_dynamic-slice_fusion = (bf16[16,2,128,128]{3,2,1,0:T(8,128)(2,1)}, bf16[16,2,128,128]{3,2,1,0:T(8,128)(2,1)}) fusion(bf16[32,2,128,128]{3,2,1,0:T(8,128)(2,1)S(1)} %get-tuple-element.16.kv_ref, s32[]{:T(128)S(6)} %select_n.15, s32[]{:T(128)S(6)} %select_n.14), kind=kLoop, calls=%fused_computation.5 | loop fusion | bytes 4194312 | tf_op jit(solution)/shard_map/dynamic_slice | solution.py:233
  76.1 0.0 copy-done.1
  76.1 0.0 collective-permute-start.1
  76.1 3.3 %collective-permute-start = (bf16[16,2,128,128]{3,2,1,0:T(8,128)(2,1)}, bf16[16,2,128,128]{3,2,1,0:T(8,128)(2,1)S(1)}, u32[]{:S(2)}, u32[]{:S(2)}) collective-permute-start(bf16[16,2,128,128]{3,2,1,0:T(8,128)(2,1)} %get-tuple-element.18), channel_id=1, source_target_pairs={{32,64},{96,128},{160,192},{64,32},{128,96},{192,160},{33,65},{97,... | collective-permute-start | bytes 3145736 | tf_op jit(solution)/shard_map/ppermute | solution.py:237
  79.4 0.1 pad_add_fusion.place_ref
  79.5 0.1 pad_add_fusion.1.place_ref
  79.5 12.4 %all-to-all-done.3.q_ref = bf16[32,128,128]{2,1,0:T(8,128)(2,1)S(1)} async-done(((bf16[32,128,128]{2,1,0:T(8,128)(2,1)}), bf16[32,128,128]{2,1,0:T(8,128)(2,1)S(1)}, u32[]{:S(2)}, u32[]{:S(2)}) %all-to-all-start.3) | async-done | bytes 1048608 | tf_op jit(solution)/shard_map/all_to_all | solution.py:217
  92.0 0.0 copy-done
  92.0 9.0 %shard_map.65.sums_ref = f32[32,128,256]{2,1,0:T(8,128)S(1)} custom-call(s32[1,3]{1,0:T(1,128)S(1)} %copy-done, bf16[32,128,128]{2,1,0:T(8,128)(2,1)S(1)} %all-to-all-done.3.q_ref, bf16[32,2,128,128]{3,2,1,0:T(8,128)(2,1)} %copy-done.1), custom_call_target="tpu_custom_call" | custom-call | flops 5033164800 | bytes 8388608 | tf_op jit(solution)/shard_map/pallas_call | solution.py:188
  101.0 0.0 collective-permute-done.1.halo_ref
  101.0 2.7 %shard_map.66.results_0_ = bf16[32,128,128]{2,1,0:T(8,128)(2,1)S(1)} custom-call(s32[2]{0:T(128)S(1)} %pad_add_fusion.1.place_ref, s32[1,3]{1,0:T(1,128)S(1)} %copy-done, bf16[32,128,128]{2,1,0:T(8,128)(2,1)S(1)} %all-to-all-done.3.q_ref, bf16[16,2,128,128]{3,2,1,0:T(8,128)(2,1)S(1)} %collective-permute-done.1.halo_ref, f32[32,128,256]{2,1,0:T(8,128)S(1)} %shard_map.65.sums_ref), custom_call_target="tpu_custom_call" | custom-call | tf_op jit(solution)/shard_map/pallas_call | solution.py:201
  103.8 0.0 collective-permute-done.halo_ref
  103.8 2.8 %shard_map.67 = bf16[32,128,128]{2,1,0:T(8,128)(2,1)S(1)} custom-call(s32[2]{0:T(128)S(1)} %pad_add_fusion.place_ref, s32[1,3]{1,0:T(1,128)S(1)} %copy-done, bf16[32,128,128]{2,1,0:T(8,128)(2,1)S(1)} %all-to-all-done.3.q_ref, bf16[16,2,128,128]{3,2,1,0:T(8,128)(2,1)S(1)} %collective-permute-done.halo_ref, f32[32,128,256]{2,1,0:T(8,128)S(1)} %shard_map.65.sums_ref, ...), custom_call_target="tpu_custom_call" | custom-call | flops 1258291200 | bytes 4194304 | tf_op jit(solution)/shard_map/pallas_call | solution.py:201
  106.6 26.9 %all_to_all.25.heads_ref = bf16[32,128,128]{2,1,0:T(8,128)(2,1)S(1)} all-to-all(bf16[32,128,128]{2,1,0:T(8,128)(2,1)S(1)} %shard_map.67), channel_id=1, replica_groups=mesh['slab'=8,'head'=32] {'head'}, dimensions={0} | all-to-all | bytes 2097152 | tf_op jit(solution)/shard_map/all_to_all | solution.py:217
  133.5 1.1 shard_map.68
Async XLA Ops:
  69.5 6.5 %copy-start.1 = (bf16[32,2,128,128]{3,2,1,0:T(8,128)(2,1)}, bf16[32,2,128,128]{3,2,1,0:T(8,128)(2,1)S(1)}, u32[]{:S(2)}) copy-start(bf16[32,2,128,128]{3,2,1,0:T(8,128)(2,1)S(1)} %get-tuple-element.16.kv_ref) | copy-start | bytes 6291460
  69.6 22.4 %all-to-all-start.3 = ((bf16[32,128,128]{2,1,0:T(8,128)(2,1)}), bf16[32,128,128]{2,1,0:T(8,128)(2,1)S(1)}, u32[]{:S(2)}, u32[]{:S(2)}) async-start(bf16[32,128,128]{2,1,0:T(8,128)(2,1)} %get-tuple-element.14), calls=%async_computation.3 | async-start | bytes 2097152 | tf_op jit(solution)/shard_map/all_to_all | solution.py:217
  74.6 17.4 %copy-start = (s32[1,3]{1,0:T(1,128)S(1)}, s32[1,3]{1,0:T(1,128)}, u32[]{:S(2)}) copy-start(s32[1,3]{1,0:T(1,128)} %windows_ref.5) | copy-start | bytes 40
  76.1 25.0 %collective-permute-start.1 = (bf16[16,2,128,128]{3,2,1,0:T(8,128)(2,1)}, bf16[16,2,128,128]{3,2,1,0:T(8,128)(2,1)S(1)}, u32[]{:S(2)}, u32[]{:S(2)}) collective-permute-start(bf16[16,2,128,128]{3,2,1,0:T(8,128)(2,1)} %get-tuple-element.17), channel_id=1, source_target_pairs={{0,32},{64,96},{128,160},{192,224},{32,0},{96,64},{160,128},{224,1... | collective-permute-start | bytes 3145736 | tf_op jit(solution)/shard_map/ppermute | solution.py:237
  76.1 27.7 %collective-permute-start = (bf16[16,2,128,128]{3,2,1,0:T(8,128)(2,1)}, bf16[16,2,128,128]{3,2,1,0:T(8,128)(2,1)S(1)}, u32[]{:S(2)}, u32[]{:S(2)}) collective-permute-start(bf16[16,2,128,128]{3,2,1,0:T(8,128)(2,1)} %get-tuple-element.18), channel_id=1, source_target_pairs={{32,64},{96,128},{160,192},{64,32},{128,96},{192,160},{33,65},{97,... | collective-permute-start | bytes 3145736 | tf_op jit(solution)/shard_map/ppermute | solution.py:237
